TPU v7x, 32 devices: a whole 2x2x4 slice. The times are simulated.
32 devices in a mesh: head: 2 (over x), blk: 16 (over z, y, core).
Axes of the slice: x: 2, y: 2, z: 4, core: 2. Of those that a mesh axis runs over, the one named last changes fastest.
Arguments:
- tokens: bfloat16 [4096, 1280], P(('head', 'blk')), may hold values from -6 to 6
- cotangent: bfloat16 [4096, 1280], P(('head', 'blk')), may hold values from -6 to 6
- permutation: int32 [4096], replicated, may hold values from 0 to 4095, as said below
- seq_lengths: int32 [8], replicated, may hold values from 1 to 2048, 4096 in all
- first_gain: bfloat16 [1280], P(('head', 'blk')), may hold values from 0.5 to 1.5
- first_bias: bfloat16 [1280], P(('head', 'blk')), may hold values from -4 to 4
- query_weight: bfloat16 [1280, 1280], P(('head', 'blk')), may hold values from -0.15625 to 0.15625
- query_bias: bfloat16 [1280], P(('head', 'blk')), may hold values from -6 to 6
- key_weight: bfloat16 [1280, 1280], P(('head', 'blk')), may hold values from -0.15625 to 0.15625
- value_weight: bfloat16 [1280, 1280], P(('head', 'blk')), may hold values from -0.15625 to 0.15625
- value_bias: bfloat16 [1280], P(('head', 'blk')), may hold values from -1.5 to 1.5
- output_weight: bfloat16 [1280, 1280], P(('head', 'blk')), may hold values from -1 to 1
- output_bias: bfloat16 [1280], P(('head', 'blk')), may hold values from -4 to 4
- second_gain: bfloat16 [1280], P(('head', 'blk')), may hold values from 0.5 to 1.5
- second_bias: bfloat16 [1280], P(('head', 'blk')), may hold values from -4 to 4
- expand_weight: bfloat16 [1280, 1280], P(('head', 'blk')), may hold values from -0.15625 to 0.15625
- expand_bias: bfloat16 [1280], P(('head', 'blk')), may hold values from -4 to 4
- contract_weight: bfloat16 [1280, 1280], P(('head', 'blk')), may hold values from -0.15625 to 0.15625
- contract_bias: bfloat16 [1280], P(('head', 'blk')), may hold values from -4 to 4
Outputs:
- mixed: bfloat16 [4096, 1280], P(('head', 'blk'))
- grad_tokens: bfloat16 [4096, 1280], P(('head', 'blk'))
- grad_first_gain: float32 [1280], P(('head', 'blk'))
- grad_first_bias: float32 [1280], P(('head', 'blk'))
- grad_query_weight: float32 [1280, 1280], P(('head', 'blk'))
- grad_query_bias: float32 [1280], P(('head', 'blk'))
- grad_key_weight: float32 [1280, 1280], P(('head', 'blk'))
- grad_value_weight: float32 [1280, 1280], P(('head', 'blk'))
- grad_value_bias: float32 [1280], P(('head', 'blk'))
- grad_output_weight: float32 [1280, 1280], P(('head', 'blk'))
- grad_output_bias: float32 [1280], P(('head', 'blk'))
- grad_second_gain: float32 [1280], P(('head', 'blk'))
- grad_second_bias: float32 [1280], P(('head', 'blk'))
- grad_expand_weight: float32 [1280, 1280], P(('head', 'blk'))
- grad_expand_bias: float32 [1280], P(('head', 'blk'))
- grad_contract_weight: float32 [1280, 1280], P(('head', 'blk'))
- grad_contract_bias: float32 [1280], P(('head', 'blk'))
Inputs may be any that keep to these rules, and one draw needn't show every extreme that they name: A permutation of all token indices. Cut the initial order and the positions into runs of 128, numbered from 0: a token never leaves its group of runs (runs r with equal r % 16), and each run of positions holds exactly 64 tokens of every run of initial tokens in its group. `seq_lengths`: sequences lie end to end in the initial order.
All inputs are finite; a program needn't handle non-finite values.
Results may differ from a plain program's by a relative error of at most 0.025.
Values may be sent and summed in bfloat16 or wider, within the bound.
A program may use at most 192 MiB of HBM per device.

v0:
```python
import jax
import jax.numpy as jnp
from jax import lax
from jax.sharding import PartitionSpec as P

HEAD_DIM = 160


def shifted(array, axis, by):
    length = lax.axis_size(axis)
    return lax.ppermute(array, axis, [(i, (i + by) % length) for i in range(length)])


def normalize(values, gain, shift):
    centre = jnp.mean(values, axis=-1, keepdims=True)
    spread = jnp.mean((values - centre) ** 2, axis=-1, keepdims=True)
    return (values - centre) * lax.rsqrt(spread + 1e-05) * gain + shift


def exact_gelu(values):
    return jax.nn.gelu(values, approximate=False)


def layout_initial(permutation, blk_source, width, blk_count, head_count):
    rows = jnp.arange(width * head_count, dtype=jnp.int32)
    places = (rows // width * blk_count + blk_source) * width + rows % width
    return jnp.take(permutation, places)


def segment_of(initial, ends):
    return jnp.sum((initial[:, None] >= ends[None, :]).astype(jnp.int32), axis=1)


def permitted(query_orig, key_orig, ends):
    same = segment_of(query_orig, ends)[:, None] == segment_of(key_orig, ends)[None, :]
    return same & (key_orig[None, :] <= query_orig[:, None])


def outer_sum(left, right):
    return lax.dot_general(
        left, right, (((0,), (0,)), ((), ())), preferred_element_type=jnp.float32
    )


def back_product(left, right):
    return lax.dot_general(
        left, right, (((1,), (1,)), ((), ())), preferred_element_type=jnp.float32
    )


def block_terms(
    query_block,
    grad_block,
    log_block,
    agree_block,
    query_orig,
    key_block,
    value_block,
    key_orig,
    ends,
    scale,
):
    allowed = permitted(query_orig, key_orig, ends)
    scores = (
        jnp.einsum("qhd,khd->hqk", query_block, key_block, preferred_element_type=jnp.float32)
        * scale
    )
    weights = jnp.exp(jnp.where(allowed[None], scores - log_block[..., None], -1e30))
    value_term = jnp.einsum(
        "hqk,qhd->khd", weights.astype(jnp.bfloat16), grad_block, preferred_element_type=jnp.float32
    )
    product = jnp.einsum(
        "qhd,khd->hqk", grad_block, value_block, preferred_element_type=jnp.float32
    )
    score_grad = (weights * (product - agree_block[..., None])).astype(jnp.bfloat16)
    query_term = jnp.einsum(
        "hqk,khd->qhd", score_grad, key_block, preferred_element_type=jnp.float32
    )
    key_term = jnp.einsum(
        "hqk,qhd->khd", score_grad, query_block, preferred_element_type=jnp.float32
    )
    return (query_term, key_term, value_term)


def local(
    tokens,
    cotangent,
    permutation,
    seq_lengths,
    first_gain,
    first_bias,
    query_weight,
    query_bias,
    key_weight,
    value_weight,
    value_bias,
    output_weight,
    output_bias,
    second_gain,
    second_bias,
    expand_weight,
    expand_bias,
    contract_weight,
    contract_bias,
):
    width = tokens.shape[0]
    blk_count = lax.axis_size("blk")
    head_count = lax.axis_size("head")
    blk_index = lax.axis_index("blk")
    flat_index = lax.axis_index("head") * blk_count + blk_index
    ends = jnp.cumsum(seq_lengths)
    total = permutation.shape[0]
    numbers = jnp.arange(total, dtype=jnp.int32)
    inverse = jnp.zeros((total,), jnp.int32).at[permutation].set(numbers)
    local_rows = jnp.arange(width, dtype=jnp.int32)
    first_row = flat_index * width
    going = lax.dynamic_slice_in_dim(inverse, first_row, width)
    order_source = jnp.argsort(going)
    arriving = lax.dynamic_slice_in_dim(permutation, first_row, width)
    order_target = jnp.argsort(arriving // width // blk_count * width + local_rows)
    undo_target = jnp.argsort(order_target)
    undo_source = jnp.argsort(order_source)
    received = lax.all_to_all(
        jnp.take(tokens, order_source, axis=0), "head", split_axis=0, concat_axis=0, tiled=True
    )
    inputs = jnp.take(received, undo_target, axis=0).astype(jnp.float32)
    vectors = jnp.stack(
        [
            first_gain,
            first_bias,
            query_bias,
            value_bias,
            output_bias,
            second_gain,
            second_bias,
            expand_bias,
            contract_bias,
        ]
    )
    query_full, key_full, value_full, output_full, expand_full, contract_full, vector_stack = (
        lax.all_gather(query_weight, ("head", "blk"), axis=0, tiled=True),
        lax.all_gather(key_weight, ("head", "blk"), axis=0, tiled=True),
        lax.all_gather(value_weight, ("head", "blk"), axis=0, tiled=True),
        lax.all_gather(output_weight, ("head", "blk"), axis=0, tiled=True),
        lax.all_gather(expand_weight, ("head", "blk"), axis=0, tiled=True),
        lax.all_gather(contract_weight, ("head", "blk"), axis=0, tiled=True),
        lax.all_gather(vectors, ("head", "blk"), axis=1, tiled=True),
    )
    vector_full = vector_stack.astype(jnp.float32)
    first_hidden = normalize(inputs, vector_full[0], vector_full[1]).astype(jnp.bfloat16)
    queries = (
        jnp.dot(first_hidden, query_full, preferred_element_type=jnp.float32) + vector_full[2]
    ).astype(jnp.bfloat16)
    keys = jnp.dot(first_hidden, key_full, preferred_element_type=jnp.float32).astype(jnp.bfloat16)
    values = (
        jnp.dot(first_hidden, value_full, preferred_element_type=jnp.float32) + vector_full[3]
    ).astype(jnp.bfloat16)
    head_queries, head_keys, head_values = (
        lax.all_to_all(queries, "head", split_axis=1, concat_axis=0, tiled=True),
        lax.all_to_all(keys, "head", split_axis=1, concat_axis=0, tiled=True),
        lax.all_to_all(values, "head", split_axis=1, concat_axis=0, tiled=True),
    )
    rows_here = width * head_count
    feature_here = head_queries.shape[1]
    heads_here = feature_here // HEAD_DIM
    scale = HEAD_DIM ** (-0.5)
    query_initial = layout_initial(permutation, blk_index, width, blk_count, head_count)
    shaped_queries = head_queries.reshape(rows_here, heads_here, HEAD_DIM)
    shaped_keys = head_keys.reshape(rows_here, heads_here, HEAD_DIM)
    shaped_values = head_values.reshape(rows_here, heads_here, HEAD_DIM)
    start_state = (
        jnp.full((heads_here, rows_here), -1e30, jnp.float32),
        jnp.zeros((heads_here, rows_here), jnp.float32),
        jnp.zeros((heads_here, rows_here, HEAD_DIM), jnp.float32),
    )
    carry = start_state
    key_piece = lax.all_gather(head_keys, "blk", axis=0, tiled=True)
    value_piece = lax.all_gather(head_values, "blk", axis=0, tiled=True)
    pieces = key_piece.shape[0] // rows_here
    key_blocks = key_piece.reshape(pieces, rows_here, heads_here, HEAD_DIM)
    value_blocks = value_piece.reshape(pieces, rows_here, heads_here, HEAD_DIM)

    def visit(state, item):
        key_block, value_block, offset = item
        running, total_sum, gathered = state
        key_initial = layout_initial(permutation, offset, width, blk_count, head_count)
        allowed = permitted(query_initial, key_initial, ends)
        scores = (
            jnp.einsum(
                "qhd,khd->hqk", shaped_queries, key_block, preferred_element_type=jnp.float32
            )
            * scale
        )
        scores = jnp.where(allowed[None], scores, -1e30)
        newest = jnp.maximum(running, jnp.max(scores, axis=-1))
        factor = jnp.exp(running - newest)
        exponent = jnp.where(allowed[None], jnp.exp(scores - newest[..., None]), 0.0)
        total_sum = factor * total_sum + jnp.sum(exponent, axis=-1)
        gathered = factor[..., None] * gathered + jnp.einsum(
            "hqk,khd->hqd",
            exponent.astype(jnp.bfloat16),
            value_block,
            preferred_element_type=jnp.float32,
        )
        return ((newest, total_sum, gathered), None)

    carry, unused = lax.scan(
        visit, carry, (key_blocks, value_blocks, jnp.arange(pieces, dtype=jnp.int32))
    )
    running, total_sum, gathered = carry
    attended = gathered / total_sum[..., None]
    log_total = running + jnp.log(total_sum)
    attended_rows = jnp.transpose(attended, (1, 0, 2)).reshape(rows_here, feature_here)
    merged = lax.all_to_all(
        attended_rows.astype(jnp.bfloat16), "head", split_axis=0, concat_axis=1, tiled=True
    )
    middle = (
        inputs + jnp.dot(merged, output_full, preferred_element_type=jnp.float32) + vector_full[4]
    )
    second_hidden = normalize(middle, vector_full[5], vector_full[6]).astype(jnp.bfloat16)
    expanded = (
        jnp.dot(second_hidden, expand_full, preferred_element_type=jnp.float32) + vector_full[7]
    )
    activated = exact_gelu(expanded).astype(jnp.bfloat16)
    result = (
        middle
        + jnp.dot(activated, contract_full, preferred_element_type=jnp.float32)
        + vector_full[8]
    )
    grad_contract = outer_sum(activated, cotangent)
    grad_contract_bias = jnp.sum(cotangent.astype(jnp.float32), axis=0)
    grad_activated = back_product(cotangent, contract_full)
    unused_value, gelu_pull = jax.vjp(exact_gelu, expanded)
    grad_expanded = gelu_pull(grad_activated)[0].astype(jnp.bfloat16)
    grad_expand = outer_sum(second_hidden, grad_expanded)
    grad_expand_bias = jnp.sum(grad_expanded.astype(jnp.float32), axis=0)
    grad_second = back_product(grad_expanded, expand_full)
    unused_second, second_pull = jax.vjp(normalize, middle, vector_full[5], vector_full[6])
    grad_middle_norm, grad_second_gain, grad_second_bias = second_pull(grad_second)
    grad_middle = cotangent.astype(jnp.float32) + grad_middle_norm
    grad_branch = grad_middle.astype(jnp.bfloat16)
    grad_output = outer_sum(merged, grad_branch)
    grad_output_bias = jnp.sum(grad_branch.astype(jnp.float32), axis=0)
    grad_merged = back_product(grad_branch, output_full).astype(jnp.bfloat16)
    head_grad = lax.all_to_all(grad_merged, "head", split_axis=1, concat_axis=0, tiled=True)
    shaped_grad = head_grad.reshape(rows_here, heads_here, HEAD_DIM)
    agreement = jnp.einsum("qhd,hqd->hq", shaped_grad.astype(jnp.float32), attended)
    zero_rows = jnp.zeros((rows_here, heads_here, HEAD_DIM), jnp.float32)

    def key_turn(turn, state):
        moving_keys, moving_values, key_total, value_total, query_total = state
        source = (blk_index - turn) % blk_count
        key_orig = layout_initial(permutation, source, width, blk_count, head_count)
        query_term, key_term, value_term = block_terms(
            shaped_queries,
            shaped_grad,
            log_total,
            agreement,
            query_initial,
            moving_keys,
            moving_values,
            key_orig,
            ends,
            scale,
        )
        moving_keys, moving_values = shifted((moving_keys, moving_values), "blk", 1)
        key_total, value_total = (
            shifted((key_total + key_term).astype(jnp.bfloat16), "blk", 1).astype(jnp.float32),
            shifted((value_total + value_term).astype(jnp.bfloat16), "blk", 1).astype(jnp.float32),
        )
        return (moving_keys, moving_values, key_total, value_total, query_total + query_term)

    final_state = lax.fori_loop(
        0, blk_count, key_turn, (shaped_keys, shaped_values, zero_rows, zero_rows, zero_rows)
    )
    key_grad_heads = final_state[2]
    value_grad_heads = final_state[3]
    query_grad_heads = final_state[4]
    query_grad_rows = (
        (query_grad_heads * scale).astype(jnp.bfloat16).reshape(rows_here, feature_here)
    )
    key_grad_rows = (key_grad_heads * scale).astype(jnp.bfloat16).reshape(rows_here, feature_here)
    value_grad_rows = value_grad_heads.astype(jnp.bfloat16).reshape(rows_here, feature_here)
    grad_queries, grad_keys, grad_values = (
        lax.all_to_all(query_grad_rows, "head", split_axis=0, concat_axis=1, tiled=True),
        lax.all_to_all(key_grad_rows, "head", split_axis=0, concat_axis=1, tiled=True),
        lax.all_to_all(value_grad_rows, "head", split_axis=0, concat_axis=1, tiled=True),
    )
    grad_query = outer_sum(first_hidden, grad_queries)
    grad_key = outer_sum(first_hidden, grad_keys)
    grad_value = outer_sum(first_hidden, grad_values)
    grad_query_bias = jnp.sum(grad_queries.astype(jnp.float32), axis=0)
    grad_value_bias = jnp.sum(grad_values.astype(jnp.float32), axis=0)
    grad_first = (
        back_product(grad_queries, query_full)
        + back_product(grad_keys, key_full)
        + back_product(grad_values, value_full)
    )
    unused_first, first_pull = jax.vjp(normalize, inputs, vector_full[0], vector_full[1])
    grad_inputs_norm, grad_first_gain, grad_first_bias = first_pull(grad_first)
    grad_inputs = (grad_middle + grad_inputs_norm).astype(jnp.bfloat16)
    vector_grads = jnp.stack(
        [
            grad_first_gain,
            grad_first_bias,
            grad_query_bias,
            grad_value_bias,
            grad_output_bias,
            grad_second_gain,
            grad_second_bias,
            grad_expand_bias,
            grad_contract_bias,
        ]
    )
    summed = (
        lax.psum_scatter(grad_query, ("head", "blk"), scatter_dimension=0, tiled=True),
        lax.psum_scatter(grad_key, ("head", "blk"), scatter_dimension=0, tiled=True),
        lax.psum_scatter(grad_value, ("head", "blk"), scatter_dimension=0, tiled=True),
        lax.psum_scatter(grad_output, ("head", "blk"), scatter_dimension=0, tiled=True),
        lax.psum_scatter(grad_expand, ("head", "blk"), scatter_dimension=0, tiled=True),
        lax.psum_scatter(grad_contract, ("head", "blk"), scatter_dimension=0, tiled=True),
        lax.psum_scatter(vector_grads, ("head", "blk"), scatter_dimension=1, tiled=True),
    )
    vector_shares = summed[6]
    returned = lax.all_to_all(
        jnp.take(grad_inputs, order_target, axis=0), "head", split_axis=0, concat_axis=0, tiled=True
    )
    grad_tokens = jnp.take(returned, undo_source, axis=0)
    return (
        result.astype(jnp.bfloat16),
        grad_tokens,
        vector_shares[0],
        vector_shares[1],
        summed[0],
        vector_shares[2],
        summed[1],
        summed[2],
        vector_shares[3],
        summed[3],
        vector_shares[4],
        vector_shares[5],
        vector_shares[6],
        summed[4],
        vector_shares[7],
        summed[5],
        vector_shares[8],
    )


def solution(mesh):
    return jax.shard_map(
        local,
        mesh=mesh,
        in_specs=(
            P(("head", "blk"), None),
            P(("head", "blk"), None),
            P(),
            P(),
            P(("head", "blk")),
            P(("head", "blk")),
            P(("head", "blk"), None),
            P(("head", "blk")),
            P(("head", "blk"), None),
            P(("head", "blk"), None),
            P(("head", "blk")),
            P(("head", "blk"), None),
            P(("head", "blk")),
            P(("head", "blk")),
            P(("head", "blk")),
            P(("head", "blk"), None),
            P(("head", "blk")),
            P(("head", "blk"), None),
            P(("head", "blk")),
        ),
        out_specs=(
            P(("head", "blk"), None),
            P(("head", "blk"), None),
            P(("head", "blk")),
            P(("head", "blk")),
            P(("head", "blk"), None),
            P(("head", "blk")),
            P(("head", "blk"), None),
            P(("head", "blk"), None),
            P(("head", "blk")),
            P(("head", "blk"), None),
            P(("head", "blk")),
            P(("head", "blk")),
            P(("head", "blk")),
            P(("head", "blk"), None),
            P(("head", "blk")),
            P(("head", "blk"), None),
            P(("head", "blk")),
        ),
        check_vma=False,
    )
```

profile of v0, /device:TPU:0, one launch (start us, length us, event | category | flops | bytes accessed | tf_op | source)
XLA Modules:
  0.0 1516.1 jit_solution(8891571572454035004)
XLA Ops:
  10.3 15.5 %scatter_custom_fusion = s32[4096]{0:T(1024)S(1)} fusion(s32[4096]{0:T(1024)S(1)} %compare_select_fusion.2, s32[4096]{0:T(1024)S(1)} %iota.48, s32[]{:T(128)} %constant.330.clone.1), kind=kCustom, calls=%fused_computation.158 | custom fusion | bytes 16388 | tf_op jit(solution)/shard_map/scatter | solution.py:114
  39.7 43.5 %all-gather = bf16[32,40,9]{1,2,0:T(8,128)(2,1)S(1)} all-gather(bf16[1,40,9]{1,2,0:T(8,128)(2,1)S(1)} %bitcast.230), channel_id=1, replica_groups=mesh['head'=2,'blk'=16] {'head','blk'}, dimensions={0}, use_global_device_ids=true | all-gather | bytes 23760 | tf_op jit(solution)/shard_map/all_gather | solution.py:147
  88.1 9.8 all_to_all.167
  97.9 38.4 %all-gather.16.cloned.1.call-done = bf16[1280,1280]{1,0:T(8,128)(2,1)} async-done(((bf16[40,1280]{1,0:T(8,128)(2,1)}), bf16[1280,1280]{1,0:T(8,128)(2,1)}) %all-gather.16.cloned.1.call-update) | async-done | bytes 3276816 | tf_op jit(solution)/shard_map/all_gather | solution.py:143
  139.0 9.7 all_to_all.168
  152.7 44.7 %all-gather.14.cloned.1.call-done = bf16[1280,1280]{1,0:T(8,128)(2,1)} async-done(((bf16[40,1280]{1,0:T(8,128)(2,1)}), bf16[1280,1280]{1,0:T(8,128)(2,1)}) %all-gather.14.cloned.1.call-update) | async-done | bytes 3276816 | tf_op jit(solution)/shard_map/all_gather | solution.py:141
  212.8 41.7 %all-gather.12.cloned.1.call-done = bf16[4096,640]{1,0:T(8,128)(2,1)} async-done(((bf16[256,640]{1,0:T(8,128)(2,1)}), bf16[4096,640]{1,0:T(8,128)(2,1)}) %all-gather.12.cloned.1.call-update) | async-done | bytes 5242896 | tf_op jit(solution)/shard_map/all_gather | solution.py:177
  254.5 16.8 %reshape.428 = bf16[16,256,4,160]{3,2,1,0:T(4,128)(2,1)} reshape(bf16[4096,640]{1,0:T(8,128)(2,1)} %all-gather.12.cloned.1.call-done) | data formatting | bytes 10485760 | tf_op jit(solution)/shard_map/reshape | solution.py:180
  271.3 13.2 copy.142
  284.5 26.7 %all-gather.18.cloned.1.call-done = bf16[4096,640]{1,0:T(8,128)(2,1)} async-done(((bf16[256,640]{1,0:T(8,128)(2,1)}), bf16[4096,640]{1,0:T(8,128)(2,1)}) %all-gather.18.cloned.1.call-update) | async-done | bytes 5242896 | tf_op jit(solution)/shard_map/all_gather | solution.py:178
  311.2 16.8 %reshape.429 = bf16[16,256,4,160]{3,2,1,0:T(4,128)(2,1)} reshape(bf16[4096,640]{1,0:T(8,128)(2,1)} %all-gather.18.cloned.1.call-done) | data formatting | bytes 10485760 | tf_op jit(solution)/shard_map/reshape | solution.py:181
  328.0 13.1 copy.143
  341.1 113.3 %while.42 = (s32[]{:T(128)}, f32[4,256]{1,0:T(4,128)S(1)}, f32[4,256]{1,0:T(4,128)S(1)}, f32[4,256,160]{1,2,0:T(8,128)S(1)}, s32[256]{0:T(256)S(1)}, /*index=5*/...) while((s32[]{:T(128)}, f32[4,256]{1,0:T(4,128)S(1)}, ...), condition=%wide.region_12.15_spmd.clone, body=%wide.region_7.14_spmd.clone.sunk | while | flops 170848256 | bytes 5786829 | solution.py:207
  458.9 9.4 all-to-all-done.4
  473.9 21.1 %all-gather.24.cloned.1.call-done = bf16[1280,1280]{1,0:T(8,128)(2,1)} async-done(((bf16[40,1280]{1,0:T(8,128)(2,1)}), bf16[1280,1280]{1,0:T(8,128)(2,1)}) %all-gather.24.cloned.1.call-update) | async-done | bytes 3276816 | tf_op jit(solution)/shard_map/all_gather | solution.py:146
  535.2 490.8 %while.43 = (s32[]{:T(128)}, bf16[256,4,160]{0,2,1:T(8,128)(2,1)S(1)}, bf16[256,4,160]{0,2,1:T(8,128)(2,1)}, f32[256,4,160]{0,2,1:T(8,128)}, f32[256,4,160]{0,2,...) while((s32[]{:T(128)}, ...), condition=%wide.region_21.24_spmd.clone, body=%wide.region_18.23_spmd.clone.sunk | while | flops 423123968 | bytes 18968048 | solution.py:273
  724.8 8.6 collective-permute-done.2
  1027.6 10.0 all_to_all.169
  1041.8 7.9 all_to_all.170
  1053.9 8.2 all_to_all.171
  1084.4 51.0 %all-reduce = f32[9,1280]{1,0:T(8,128)S(1)} all-reduce(f32[9,1280]{1,0:T(8,128)S(1)} %stack.67), channel_id=2, replica_groups=mesh['head'=2,'blk'=16] {'head','blk'}, use_global_device_ids=true, to_apply=%region_35.38.clone | all-reduce | flops 11520 | bytes 92160
  1137.8 82.9 %reduce-scatter.8.cloned.1.call-done = f32[40,1280]{1,0:T(8,128)} async-done(((f32[1280,1280]{1,0:T(8,128)}), f32[40,1280]{1,0:T(8,128)}) %reduce-scatter.8.cloned.1.call-update) | async-done | bytes 204816 | tf_op jit(solution)/shard_map/reduce_scatter | solution.py:316
  1220.8 144.1 %reduce-scatter.10.cloned.1.call-done = f32[40,1280]{1,0:T(8,128)} async-done(((f32[1280,1280]{1,0:T(8,128)}), f32[40,1280]{1,0:T(8,128)}) %reduce-scatter.10.cloned.1.call-update) | async-done | bytes 204816 | tf_op jit(solution)/shard_map/reduce_scatter | solution.py:317
  1364.9 144.2 %reduce-scatter.12.cloned.1.call-done = f32[40,1280]{1,0:T(8,128)} async-done(((f32[1280,1280]{1,0:T(8,128)}), f32[40,1280]{1,0:T(8,128)}) %reduce-scatter.12.cloned.1.call-update) | async-done | bytes 204816 | tf_op jit(solution)/shard_map/reduce_scatter | solution.py:318
  (807 shorter events, 721.2 us)
Async XLA Ops:
  7.3 78.1 %all-gather.10.cloned.1.call-start = ((), (), s32[]{:S(2)}) async-start(), calls=%async_computation.16 | async-start | bytes 3379200 | tf_op jit(solution)/shard_map/all_gather | solution.py:142
  8.0 128.3 %all-gather.16.cloned.1.call-start = ((), (), s32[]{:S(2)}) async-start(), calls=%async_computation.19 | async-start | bytes 3379200 | tf_op jit(solution)/shard_map/all_gather | solution.py:143
  8.8 188.6 %all-gather.14.cloned.1.call-start = ((), (), s32[]{:S(2)}) async-start(), calls=%async_computation.18 | async-start | bytes 3379200 | tf_op jit(solution)/shard_map/all_gather | solution.py:141
  30.2 53.8 %all-to-all-start = ((bf16[2,64,1280]{2,1,0:T(8,128)(2,1)}), bf16[2,64,1280]{2,1,0:T(8,128)(2,1)S(1)}, u32[]{:S(2)}, u32[]{:S(2)}) async-start(bf16[2,64,1280]{2,1,0:T(8,128)(2,1)} %bitcast.1), calls=%async_computation | async-start | bytes 655360 | tf_op jit(solution)/shard_map/all_to_all | solution.py:123
  34.4 220.1 %all-gather.12.cloned.1.call-start = ((), (), s32[]{:S(2)}) async-start(), calls=%async_computation.17 | async-start | bytes 5570560 | tf_op jit(solution)/shard_map/all_gather | solution.py:177
  97.9 213.3 %all-gather.18.cloned.1.call-start = ((), (), s32[]{:S(2)}) async-start(), calls=%async_computation.20 | async-start | bytes 5570560 | tf_op jit(solution)/shard_map/all_gather | solution.py:178
  148.7 310.2 %all-gather.20.cloned.1.call-start = ((), (), s32[]{:S(2)}) async-start(), calls=%async_computation.21 | async-start | bytes 3379200 | tf_op jit(solution)/shard_map/all_gather | solution.py:144
  149.3 322.0 %all-gather.22.cloned.1.call-start = ((), (), s32[]{:S(2)}) async-start(), calls=%async_computation.22 | async-start | bytes 3379200 | tf_op jit(solution)/shard_map/all_gather | solution.py:145
  150.0 344.9 %all-gather.24.cloned.1.call-start = ((), (), s32[]{:S(2)}) async-start(), calls=%async_computation.23 | async-start | bytes 3379200 | tf_op jit(solution)/shard_map/all_gather | solution.py:146
  458.9 679.0 %reduce-scatter.14.cloned.1.call-start = ((), (), s32[]{:S(2)}) async-start(), calls=%async_computation.27 | async-start | bytes 6758400 | tf_op jit(solution)/shard_map/reduce_scatter | solution.py:319
  507.0 630.8 %reduce-scatter.16.cloned.1.call-start = ((), (), s32[]{:S(2)}) async-start(), calls=%async_computation.28 | async-start | bytes 6758400 | tf_op jit(solution)/shard_map/reduce_scatter | solution.py:320
  526.3 611.5 %reduce-scatter.18.cloned.1.call-start = ((), (), s32[]{:S(2)}) async-start(), calls=%async_computation.29 | async-start | bytes 6758400 | tf_op jit(solution)/shard_map/reduce_scatter | solution.py:321
  532.6 688.2 %reduce-scatter.8.cloned.1.call-start = ((), (), s32[]{:S(2)}) async-start(), calls=%async_computation.24 | async-start | bytes 6758400 | tf_op jit(solution)/shard_map/reduce_scatter | solution.py:316
  544.7 21.8 %collective-permute-start.1 = (bf16[256,4,160]{0,2,1:T(8,128)(2,1)S(1)}, bf16[256,4,160]{0,2,1:T(8,128)(2,1)}, u32[]{:S(2)}, u32[]{:S(2)}) collective-permute-start(bf16[256,4,160]{0,2,1:T(8,128)(2,1)S(1)} %copy.206), channel_id=1, source_target_pairs={{0,1},{1,2},{2,3},{3,4},{4,5},{5,6},{6,7},{7,8},{8,9},{9,10},{10,1... | collective-permute-start | bytes 983048 | tf_op jit(solution)/shard_map/while/body/eval_jaxpr/ppermute | solution.py:11
  633.3 21.9 %collective-permute-start.1 = (bf16[256,4,160]{0,2,1:T(8,128)(2,1)S(1)}, bf16[256,4,160]{0,2,1:T(8,128)(2,1)}, u32[]{:S(2)}, u32[]{:S(2)}) collective-permute-start(bf16[256,4,160]{0,2,1:T(8,128)(2,1)S(1)} %copy.206), channel_id=1, source_target_pairs={{0,1},{1,2},{2,3},{3,4},{4,5},{5,6},{6,7},{7,8},{8,9},{9,10},{10,1... | collective-permute-start | bytes 983048 | tf_op jit(solution)/shard_map/while/body/eval_jaxpr/ppermute | solution.py:11
  663.2 22.5 %collective-permute-start.1 = (bf16[256,4,160]{0,2,1:T(8,128)(2,1)S(1)}, bf16[256,4,160]{0,2,1:T(8,128)(2,1)}, u32[]{:S(2)}, u32[]{:S(2)}) collective-permute-start(bf16[256,4,160]{0,2,1:T(8,128)(2,1)S(1)} %copy.206), channel_id=1, source_target_pairs={{0,1},{1,2},{2,3},{3,4},{4,5},{5,6},{6,7},{7,8},{8,9},{9,10},{10,1... | collective-permute-start | bytes 983048 | tf_op jit(solution)/shard_map/while/body/eval_jaxpr/ppermute | solution.py:11
  722.5 25.5 %collective-permute-start.1 = (bf16[256,4,160]{0,2,1:T(8,128)(2,1)S(1)}, bf16[256,4,160]{0,2,1:T(8,128)(2,1)}, u32[]{:S(2)}, u32[]{:S(2)}) collective-permute-start(bf16[256,4,160]{0,2,1:T(8,128)(2,1)S(1)} %copy.206), channel_id=1, source_target_pairs={{0,1},{1,2},{2,3},{3,4},{4,5},{5,6},{6,7},{7,8},{8,9},{9,10},{10,1... | collective-permute-start | bytes 983048 | tf_op jit(solution)/shard_map/while/body/eval_jaxpr/ppermute | solution.py:11
  756.1 22.9 %collective-permute-start.1 = (bf16[256,4,160]{0,2,1:T(8,128)(2,1)S(1)}, bf16[256,4,160]{0,2,1:T(8,128)(2,1)}, u32[]{:S(2)}, u32[]{:S(2)}) collective-permute-start(bf16[256,4,160]{0,2,1:T(8,128)(2,1)S(1)} %copy.206), channel_id=1, source_target_pairs={{0,1},{1,2},{2,3},{3,4},{4,5},{5,6},{6,7},{7,8},{8,9},{9,10},{10,1... | collective-permute-start | bytes 983048 | tf_op jit(solution)/shard_map/while/body/eval_jaxpr/ppermute | solution.py:11
  787.0 22.9 %collective-permute-start.1 = (bf16[256,4,160]{0,2,1:T(8,128)(2,1)S(1)}, bf16[256,4,160]{0,2,1:T(8,128)(2,1)}, u32[]{:S(2)}, u32[]{:S(2)}) collective-permute-start(bf16[256,4,160]{0,2,1:T(8,128)(2,1)S(1)} %copy.206), channel_id=1, source_target_pairs={{0,1},{1,2},{2,3},{3,4},{4,5},{5,6},{6,7},{7,8},{8,9},{9,10},{10,1... | collective-permute-start | bytes 983048 | tf_op jit(solution)/shard_map/while/body/eval_jaxpr/ppermute | solution.py:11
  818.0 23.0 %collective-permute-start.1 = (bf16[256,4,160]{0,2,1:T(8,128)(2,1)S(1)}, bf16[256,4,160]{0,2,1:T(8,128)(2,1)}, u32[]{:S(2)}, u32[]{:S(2)}) collective-permute-start(bf16[256,4,160]{0,2,1:T(8,128)(2,1)S(1)} %copy.206), channel_id=1, source_target_pairs={{0,1},{1,2},{2,3},{3,4},{4,5},{5,6},{6,7},{7,8},{8,9},{9,10},{10,1... | collective-permute-start | bytes 983048 | tf_op jit(solution)/shard_map/while/body/eval_jaxpr/ppermute | solution.py:11
  849.1 24.0 %collective-permute-start.1 = (bf16[256,4,160]{0,2,1:T(8,128)(2,1)S(1)}, bf16[256,4,160]{0,2,1:T(8,128)(2,1)}, u32[]{:S(2)}, u32[]{:S(2)}) collective-permute-start(bf16[256,4,160]{0,2,1:T(8,128)(2,1)S(1)} %copy.206), channel_id=1, source_target_pairs={{0,1},{1,2},{2,3},{3,4},{4,5},{5,6},{6,7},{7,8},{8,9},{9,10},{10,1... | collective-permute-start | bytes 983048 | tf_op jit(solution)/shard_map/while/body/eval_jaxpr/ppermute | solution.py:11
  1041.6 323.3 %reduce-scatter.10.cloned.1.call-start = ((), (), s32[]{:S(2)}) async-start(), calls=%async_computation.25 | async-start | bytes 6758400 | tf_op jit(solution)/shard_map/reduce_scatter | solution.py:317
  1053.7 455.5 %reduce-scatter.12.cloned.1.call-start = ((), (), s32[]{:S(2)}) async-start(), calls=%async_computation.26 | async-start | bytes 6758400 | tf_op jit(solution)/shard_map/reduce_scatter | solution.py:318
  1080.4 55.7 %all-to-all-start.9 = ((bf16[2,64,1280]{2,1,0:T(8,128)(2,1)}), bf16[2,64,1280]{2,1,0:T(8,128)(2,1)S(1)}, u32[]{:S(2)}, u32[]{:S(2)}) async-start(bf16[2,64,1280]{2,1,0:T(8,128)(2,1)} %bitcast.32), calls=%async_computation.9 | async-start | bytes 655360 | tf_op jit(solution)/shard_map/all_to_all | solution.py:325
  (94 other events, 1885.6 us)
Sparse Core Ops, SparseCore 0:
  11.0 64.0 all-gather.9
  78.0 58.3 all-gather.15
  139.2 58.1 all-gather.13
  199.5 54.8 all-gather.11
  256.6 54.5 all-gather.17
  313.9 57.8 all-gather.19
  374.6 58.2 all-gather.21
  435.8 59.0 all-gather.23
  507.2 179.1 reduce-scatter.13
  689.1 204.0 reduce-scatter.15
  896.1 178.0 reduce-scatter.17
  1076.9 143.8 reduce-scatter.7
  1223.6 141.2 reduce-scatter.9
  1367.6 141.4 reduce-scatter.11
where the time goes:
time: 1530 us; the launch traced here: 1520 us
  waiting for transfers between devices  817 us (53%)
  matrix products  217 us (14%)
  local copies, waits for them, and re-layouts  179 us (12%)
  blocking collectives  140 us (9%)
  other arithmetic  99.1 us (6%)
  starting transfers between devices  46.6 us (3%)
    ppermute x64, waiting for transfers between devices, shifted(): lax.ppermute(array, axis, [(i, (i + by) % length) for i in range(length)])  252 us
    reduce_scatter x1, waiting for transfers between devices, local(): lax.psum_scatter(grad_value, ('head', 'blk'), scatter_dimension=0, tiled=...  144 us
    reduce_scatter x1, waiting for transfers between devices, local(): lax.psum_scatter(grad_key, ('head', 'blk'), scatter_dimension=0, tiled=True)  144 us
    reduce_scatter x1, waiting for transfers between devices, local(): lax.psum_scatter(grad_query, ('head', 'blk'), scatter_dimension=0, tiled=...  82.9 us
    gather x33, local copies, waits for them, and re-layouts, layout_initial(): return jnp.take(permutation, places)  56.8 us
    unnamed x1, blocking collectives  51 us
    all_gather x1, waiting for transfers between devices, local(): lax.all_gather(query_weight, ('head', 'blk'), axis=0, tiled=True)  44.7 us
    all_gather x1, blocking collectives, local(): lax.all_gather(vectors, ('head', 'blk'), axis=1, tiled=True)  43.5 us
  transfers between devices with their start and end apart: 83, of which 73 were waited for; matrix products, arithmetic and copies ran while one was open for 32% of the time, Pallas kernels for 0%

commit v1 on v0

--- a/solution.py
+++ b/solution.py
@@ -1,9 +1,784 @@
+import functools
 import jax
 import jax.numpy as jnp
 from jax import lax
+from jax.experimental import pallas as pl
+from jax.experimental.pallas import tpu as pltpu
 from jax.sharding import PartitionSpec as P
 
 HEAD_DIM = 160
+MESH = pl.DeviceIdType.MESH
+BF = jnp.bfloat16
+F32 = jnp.float32
+MB = 1 << 20
+
+
+def nn(a, b):
+    return lax.dot_general(a, b, (((1,), (0,)), ((), ())), preferred_element_type=F32)
+
+
+def nt(a, b):
+    return lax.dot_general(a, b, (((1,), (1,)), ((), ())), preferred_element_type=F32)
+
+
+def tn(a, b):
+    return lax.dot_general(a, b, (((0,), (0,)), ((), ())), preferred_element_type=F32)
+
+
+def stats(v):
+    centre = jnp.mean(v, axis=-1, keepdims=True)
+    off = v - centre
+    spread = jnp.mean(off * off, axis=-1, keepdims=True)
+    r = lax.rsqrt(spread + 1e-05)
+    return off * r, r
+
+
+def block_kernel(
+    tok, cot, perm2, lens, wpre, fpre,
+    mixed_out, gtok_out, fout, wout,
+    T, H, W, KV, Q, O, F, G, R0, R1, R2, R3, FA, FR,
+    wr, wasm, fr, colb, vec, bias,
+    LS, ST, A, As, C, RES, MID, N2, RR, EX, H2, ACT, CI, DE, GB, DOs, DOr,
+    DK, DV, DQ, DKVr, DKVQ, U, UR, UZ, VR, VS, DW, DWr, DWz, DWh, WOr,
+    ss, rs,
+):
+    h = lax.axis_index("head")
+    b = lax.axis_index("blk")
+    z = lax.div(b, 4)
+    y = lax.rem(lax.div(b, 2), 2)
+    c = lax.rem(b, 2)
+    sib = 1 - c
+    hx = 1 - h
+    yx = 1 - y
+    t = z * 2 + c
+    first = c == 0
+    p1h = jnp.where(first, hx, h)
+    p1y = jnp.where(first, y, yx)
+    p2h = jnp.where(first, h, hx)
+    p2y = jnp.where(first, yx, y)
+
+    def dev(hh, zz, yy, cc):
+        return (hh, zz * 4 + yy * 2 + cc)
+
+    zs = [lax.rem(z + k, 4) for k in range(4)]
+    zr = [lax.rem(z + 4 - k, 4) for k in range(4)]
+    SIB = dev(h, z, y, sib)
+    P1 = dev(p1h, z, p1y, c)
+    P2 = dev(p2h, z, p2y, c)
+    XP = dev(hx, z, y, c)
+    YP = dev(h, z, yx, c)
+    DP = dev(hx, z, yx, c)
+    plane = [(h, yx, YP), (hx, y, XP), (hx, yx, DP)]
+
+    count = [0]
+
+    def desc(src, dst, device):
+        i = count[0]
+        count[0] += 1
+        return pltpu.make_async_remote_copy(
+            src_ref=src, dst_ref=dst, send_sem=ss.at[i], recv_sem=rs.at[i],
+            device_id=device, device_id_type=MESH,
+        )
+
+    pending = []
+
+    def send(src, dst, device):
+        cp = desc(src, dst, device)
+        cp.start()
+        pending.append(cp)
+        return cp
+
+    def left(cps):
+        for cp in cps:
+            cp.wait_send()
+        keep = [cp for cp in pending if not any(cp is one for one in cps)]
+        pending[:] = keep
+
+    bar = pltpu.get_barrier_semaphore()
+    for k in range(1, 4):
+        pl.semaphore_signal(bar, inc=1, device_id=dev(h, zs[k], y, c), device_id_type=MESH)
+        pl.semaphore_signal(bar, inc=1, device_id=dev(h, zs[k], y, sib), device_id_type=MESH)
+    for peer in (SIB, XP, YP, DP):
+        pl.semaphore_signal(bar, inc=1, device_id=peer, device_id_type=MESH)
+    pl.semaphore_wait(bar, 10)
+
+    wa = send(wpre.at[sib], wr, SIB)
+    fa = send(fpre.at[sib], fr, SIB)
+    tz = [send(tok, T.at[z, c], dev(h, zs[k], y, c)) for k in range(1, 4)]
+    ts = [send(tok, T.at[z, c], SIB)]
+    cx = send(cot, C.at[h], XP)
+    T[z, c] = tok[...]
+    C[h] = cot[...]
+
+    wa.wait_recv()
+    wasm[:, pl.ds(pl.multiple_of(c * 40, 8), 40), :] = wpre[c]
+    wasm[:, pl.ds(pl.multiple_of(sib * 40, 8), 40), :] = wr[...]
+    for k in range(4):
+        DWz[k] = wasm[k].astype(BF)
+    W[h, z, y] = DWz[z]
+    wz = [send(DWz.at[zs[k]], W.at[h, z, y], dev(h, zs[k], y, c)) for k in range(1, 4)]
+    fa.wait_recv()
+    FA[:, pl.ds(pl.multiple_of(c * 40, 8), 40), :] = fpre[c]
+    FA[:, pl.ds(pl.multiple_of(sib * 40, 8), 40), :] = fr[...]
+    for w in range(3):
+        F[w, c, h, z, y] = FA[w].astype(BF)
+    for cp in wz:
+        cp.wait_recv()
+    wp = [send(W.at[h, :, y], W.at[h, :, y], d) for (_, _, d) in plane]
+    fz = [
+        [send(F.at[w, c, h, z, y], F.at[w, c, h, z, y], dev(h, zs[k], y, c)) for k in range(1, 4)]
+        for w in range(3)
+    ]
+    for k in range(1, 4):
+        tz[k - 1].wait_recv()
+        ts.append(send(T.at[zr[k], c], T.at[zr[k], c], SIB))
+    for cp in wp:
+        cp.wait_recv()
+
+    def tcol(hh, _):
+        colb[pl.ds(pl.multiple_of(hh * 640, 128), 640), :] = (
+            W[hh, :, :, :, 384:512].reshape(640, 128).astype(F32)
+        )
+        return 0
+
+    lax.fori_loop(0, 2, tcol, 0)
+    colb[1280:1408, :] = jnp.zeros((128, 128), F32)
+    vec[...] = jnp.transpose(colb[0:1280, :])[96:112, :]
+    mine = jnp.transpose(colb[pl.ds(pl.multiple_of(t * 160, 8), 256), :])
+    bias[...] = jnp.zeros((8, 512), F32)
+    bias[0:1, 160:320] = mine[99:100, 0:160]
+    bias[0:1, 320:480] = mine[98:99, 0:160]
+
+    lane256 = lax.broadcasted_iota(jnp.int32, (256, 256), 1)
+
+    kv_y, kv_x, kv_d = [], [], []
+    for k in range(4):
+        zt = zr[k]
+        ts[k].wait_recv()
+
+        def norm(i, _):
+            rows = pl.ds(pl.multiple_of(lax.rem(i, 2) * 64, 64), 64)
+            n, _ = stats(T[zt, lax.div(i, 2), rows].astype(F32))
+            H[zt, pl.ds(pl.multiple_of(i * 64, 64), 64)] = (n * vec[0:1, :] + vec[1:2, :]).astype(BF)
+            return 0
+
+        lax.fori_loop(0, 4, norm, 0)
+        kvq = nn(H[zt], W[...].reshape(1280, 512)) + bias[0:1, :]
+        KV[h, zt, y] = kvq[:, 0:384].astype(BF)
+        qr = pltpu.roll(kvq[:, 256:512], 192, 1)
+        Q[zt] = jnp.where(lane256 < 160, qr, 0.0).astype(BF)
+        src = KV.at[h, zt, y]
+        kv_y.append(send(src, KV.at[h, zt, y], YP))
+        cpx = desc(src, KV.at[h, zt, y], XP)
+        cpd = desc(src, KV.at[h, zt, y], DP)
+        kv_x.append(cpx)
+        kv_d.append(cpd)
+
+        @pl.when(h == 0)
+        def _():
+            cpx.start()
+            cpd.start()
+
+    f1, f2a, fs = [], [], []
+    for w in range(3):
+        for cp in fz[w]:
+            cp.wait_recv()
+        own = F.at[w, c, h, :, y]
+        f1.append(send(own, own, P1))
+        f2a.append(send(own, own, P2))
+        fs.append(send(own, own, SIB))
+
+    for cp in kv_y:
+        cp.wait_recv()
+
+    @pl.when(h == 1)
+    def _():
+        for cp in kv_x + kv_d:
+            cp.wait_recv()
+
+    f2b = []
+    for w in range(3):
+        f1[w].wait_recv()
+        got = F.at[w, c, p1h, :, p1y]
+        f2b.append(send(got, got, P2))
+        fs.append(send(got, got, SIB))
+
+    scale = HEAD_DIM ** -0.5
+    ends = []
+    run = 0
+    for e in range(8):
+        run = run + lens[e]
+        ends.append(run)
+
+    def seg_of(pos):
+        s = jnp.zeros_like(pos)
+        for e in range(7):
+            s = jnp.where(pos >= ends[e], ends[e], s)
+        return s
+
+    def rowpos(zt):
+        return (h * 8 + zt * 2 + y) * 256
+
+    def fwd_tile(zt, _):
+        qt = h * 8 + zt * 2 + y
+        lo = jnp.maximum(qt - 8, 0)
+        num = qt + 1 - lo
+        qpos = qt * 256 + lax.broadcasted_iota(jnp.int32, (256, 1), 0)
+        seg = seg_of(qpos)
+        q = Q[zt]
+
+        def score(j, ml):
+            m, l = ml
+            kt = lo + j
+            kh, kz, ky = lax.div(kt, 8), lax.rem(lax.div(kt, 2), 4), lax.rem(kt, 2)
+            s = nt(q, KV[kh, kz, ky, :, 0:256]) * scale
+            kpos = kt * 256 + lax.broadcasted_iota(jnp.int32, (256, 256), 1)
+            ok = (kpos >= seg) & (kpos <= qpos)
+            s = jnp.where(ok, s, -1e30)
+            mn = jnp.maximum(m, jnp.max(s, axis=-1, keepdims=True))
+            f = jnp.exp(m - mn)
+            p = jnp.where(ok, jnp.exp(s - mn), 0.0)
+            O[zt] = O[zt] * f + nn(p.astype(BF), KV[kh, kz, ky, :, 128:384])
+            return mn, l * f + jnp.sum(p, axis=-1, keepdims=True)
+
+        O[zt] = jnp.zeros((256, 256), F32)
+        start = (jnp.full((256, 1), -1e30, F32), jnp.zeros((256, 1), F32))
+        m, l = lax.fori_loop(0, num, score, start)
+        o = O[zt] / l
+        O[zt] = o
+        LS[zt] = jnp.broadcast_to(m + jnp.log(l), (256, 128))
+        a = pltpu.roll(o, 224, 1).astype(BF)
+        As[zt] = a.reshape(2, 128, 256)
+        return 0
+
+    asend = []
+    for k in (1, 2, 3, 0):
+        zt = zs[k]
+        fwd_tile(zt, 0)
+        for cc in (c, sib):
+            if k == 0 and cc is c:
+                continue
+            asend.append(send(As.at[zt, cc], A.at[t], dev(h, zt, y, cc)))
+    A[t] = As[z, c]
+
+    for w in range(3):
+        f2a[w].wait_recv()
+        got = F.at[w, c, p2h, :, p2y]
+        fs.append(send(got, got, SIB))
+        f2b[w].wait_recv()
+        got = F.at[w, c, hx, :, yx]
+        fs.append(send(got, got, SIB))
+    for cp in asend:
+        cp.wait_recv()
+    for cp in fs:
+        cp.wait_recv()
+
+    VR[...] = jnp.zeros((128, 1280), F32)
+
+    def halves(fn):
+        def run_half(i, _):
+            fn(i, pl.ds(pl.multiple_of(i * 640, 128), 640))
+            return 0
+
+        lax.fori_loop(0, 2, run_half, 0)
+
+    def out_half(i, cols):
+        acc = tok[:, cols].astype(F32) + vec[4:5, cols]
+        for e in range(8):
+            acc += nn(A[e, :, 0:160], F[0, i, e // 4, e % 4].reshape(160, 640))
+        MID[:, cols] = acc
+
+    halves(out_half)
+
+    def norm2(i, _):
+        rows = pl.ds(pl.multiple_of(i * 32, 32), 32)
+        n2, r2 = stats(MID[rows, :])
+        N2[rows, :] = n2
+        RR[rows, :] = jnp.broadcast_to(r2, (32, 128))
+        H2[rows, :] = (n2 * vec[5:6, :] + vec[6:7, :]).astype(BF)
+        return 0
+
+    lax.fori_loop(0, 4, norm2, 0)
+
+    def exp_half(i, cols):
+        ex = nn(H2[...], F[1, i].reshape(1280, 640)) + vec[7:8, cols]
+        phi = 0.5 * (1.0 + lax.erf(ex * (0.5**0.5)))
+        ACT[:, cols] = (ex * phi).astype(BF)
+        EX[:, cols] = phi + ex * jnp.exp(-0.5 * ex * ex) * 0.3989422804014327
+
+    halves(exp_half)
+
+    def con_half(i, cols):
+        res = MID[:, cols] + nn(ACT[...], F[2, i].reshape(1280, 640)) + vec[8:9, cols]
+        RES[h, :, cols] = res.astype(BF)
+
+    halves(con_half)
+    rx = send(RES.at[h], RES.at[h], XP)
+
+    cx.wait_recv()
+    i_sub = lax.broadcasted_iota(jnp.int32, (128, 128), 0)
+    mine0 = (h * 16 + b) * 128
+    oh0 = jnp.where(perm2[0:1, :] == mine0 + i_sub, 1.0, 0.0).astype(BF)
+    oh1 = jnp.where(perm2[1:2, :] == mine0 + i_sub, 1.0, 0.0).astype(BF)
+
+    def cot_half(i, cols):
+        ci = nn(oh0, C[0, :, cols]) + nn(oh1, C[1, :, cols])
+        CI[:, cols] = ci.astype(BF)
+        VR[104:105, cols] = jnp.sum(ci, axis=0, keepdims=True)
+
+    halves(cot_half)
+
+    def act_half(i, cols):
+        f0, f1w = F[2, 0, i].reshape(640, 640), F[2, 1, i].reshape(640, 640)
+        dact = nt(CI[:, 0:640], f0) + nt(CI[:, 640:1280], f1w)
+        de = (dact * EX[:, cols]).astype(BF)
+        DE[:, cols] = de
+        VR[103:104, cols] = jnp.sum(de.astype(F32), axis=0, keepdims=True)
+
+    halves(act_half)
+
+    def outer(left, right, dst):
+        def one(i, _):
+            hh, half = lax.div(i, 2), lax.rem(i, 2)
+            g = tn(
+                left[:, pl.ds(pl.multiple_of(hh * 640, 128), 640)],
+                right[:, pl.ds(pl.multiple_of(half * 640, 128), 640)],
+            )
+            dst[half, hh] = g.astype(BF).reshape(4, 2, 80, 640)
+            return 0
+
+        lax.fori_loop(0, 4, one, 0)
+
+    Gw = [F.at[1], F.at[2], G]
+    ra = [None] * 3
+
+    def rs_a(w):
+        ra[w] = send(Gw[w].at[sib], R0.at[w], SIB)
+
+    outer(ACT, CI, G)
+    rs_a(2)
+
+    def back_half(i, cols):
+        f0, f1w = F[1, 0, i].reshape(640, 640), F[1, 1, i].reshape(640, 640)
+        EX[:, cols] = nt(DE[:, 0:640], f0) + nt(DE[:, 640:1280], f1w)
+
+    halves(back_half)
+
+    def norm2_back(i, _):
+        rows = pl.ds(pl.multiple_of(i * 32, 32), 32)
+        dh2, n2 = EX[rows, :], N2[rows, :]
+        VR[101:102, :] += jnp.sum(dh2 * n2, axis=0, keepdims=True)
+        VR[102:103, :] += jnp.sum(dh2, axis=0, keepdims=True)
+        wv = dh2 * vec[5:6, :]
+        dmid = CI[rows, :].astype(F32) + RR[rows, 0:1] * (
+            wv - jnp.mean(wv, axis=-1, keepdims=True) - n2 * jnp.mean(wv * n2, axis=-1, keepdims=True)
+        )
+        MID[rows, :] = dmid
+        gb = dmid.astype(BF)
+        GB[rows, :] = gb
+        VR[100:101, :] += jnp.sum(gb.astype(F32), axis=0, keepdims=True)
+        return 0
+
+    lax.fori_loop(0, 4, norm2_back, 0)
+    left(asend)
+    As[...] = jnp.zeros((4, 2, 128, 256), BF)
+
+    def dattn(e, _):
+        eh, ez = lax.div(e, 4), lax.rem(e, 4)
+        da = nt(GB[:, 0:640], F[0, 0, eh, ez].reshape(160, 640)) + nt(
+            GB[:, 640:1280], F[0, 1, eh, ez].reshape(160, 640)
+        )
+        As[lax.div(e, 2), lax.rem(e, 2), :, 0:160] = da.astype(BF)
+        return 0
+
+    lax.fori_loop(0, 8, dattn, 0)
+    dos = []
+    for k in range(4):
+        for cc in (c, sib):
+            if k == 0 and cc is c:
+                continue
+            dos.append(send(As.at[zs[k], cc], DOr.at[z, c], dev(h, zs[k], y, cc)))
+    DOr[z, c] = As[z, c]
+
+    left([cp for row in fz for cp in row] + f1 + f2a + f2b + fs)
+    outer(H2, DE, F.at[2])
+    rs_a(1)
+
+    def outo(e, _):
+        def one(half, _):
+            g = tn(A[e, :, 0:160], GB[:, pl.ds(pl.multiple_of(half * 640, 128), 640)])
+            F[1, half, lax.div(e, 4), lax.rem(e, 4)] = g.astype(BF).reshape(2, 80, 640)
+            return 0
+
+        lax.fori_loop(0, 2, one, 0)
+        return 0
+
+    lax.fori_loop(0, 8, outo, 0)
+    rs_a(0)
+
+    rx.wait_recv()
+    pm = jnp.where(h == 0, perm2[0:1, :], perm2[1:2, :])
+    om0 = jnp.where(pm == b * 128 + i_sub, 1.0, 0.0).astype(BF)
+    om1 = jnp.where(pm == (16 + b) * 128 + i_sub, 1.0, 0.0).astype(BF)
+
+    def mix_half(i, cols):
+        mixed_out[:, cols] = (tn(om0, RES[0, :, cols]) + tn(om1, RES[1, :, cols])).astype(BF)
+
+    halves(mix_half)
+
+    def add_into(dst_at, others):
+        def one(i, _):
+            ref, idx = dst_at(i)
+            total = ref[idx].astype(F32)
+            for other in others:
+                total += other(i).astype(F32)
+            ref[idx] = total.astype(BF)
+            return 0
+
+        return one
+
+    r1, r2s, r3, r4 = [None] * 3, [None] * 3, [None] * 3, [None] * 3
+
+    def rs_b(w):
+        ra[w].wait_recv()
+        gw = Gw[w]
+
+        def one(i, _):
+            ih, iz = lax.div(i, 4), lax.rem(i, 4)
+            gw[c, ih, iz] = (gw[c, ih, iz].astype(F32) + R0[w, ih, iz].astype(F32)).astype(BF)
+            return 0
+
+        lax.fori_loop(0, 8, one, 0)
+        r1[w] = [
+            send(gw.at[c, hx, :, yx], R1.at[w, 1], P2),
+            send(gw.at[c, p2h, :, p2y], R1.at[w, 0], P2),
+        ]
+
+    def rs_c(w):
+        gw = Gw[w]
+        for cp in r1[w]:
+            cp.wait_recv()
+
+        def one(i, _):
+            gw[c, p1h, i, p1y] = (gw[c, p1h, i, p1y].astype(F32) + R1[w, 1, i].astype(F32)).astype(BF)
+            return 0
+
+        lax.fori_loop(0, 4, one, 0)
+        r2s[w] = send(gw.at[c, p1h, :, p1y], R2.at[w], P1)
+
+    def rs_d(w):
+        gw = Gw[w]
+        r2s[w].wait_recv()
+
+        def two(i, _):
+            gw[c, h, i, y] = (
+                gw[c, h, i, y].astype(F32) + R1[w, 0, i].astype(F32) + R2[w, i].astype(F32)
+            ).astype(BF)
+            return 0
+
+        lax.fori_loop(0, 4, two, 0)
+        r3[w] = [send(gw.at[c, h, zs[k], y], R3.at[w, k - 1], dev(h, zs[k], y, c)) for k in range(1, 4)]
+
+    def rs_e(w):
+        gw = Gw[w]
+        total = gw[c, h, z, y].astype(F32)
+        for k in range(1, 4):
+            r3[w][k - 1].wait_recv()
+            total += R3[w, k - 1].astype(F32)
+        FA[w] = total
+        r4[w] = send(FA.at[w, pl.ds(pl.multiple_of(sib * 40, 8), 40)], FR.at[w], SIB)
+
+    def rs_f(w):
+        r4[w].wait_recv()
+        fout[w, :, pl.ds(pl.multiple_of(c * 640, 128), 640)] = FA[w, pl.ds(pl.multiple_of(c * 40, 8), 40)]
+        fout[w, :, pl.ds(pl.multiple_of(sib * 640, 128), 640)] = FR[w]
+
+    for w in (2, 1, 0):
+        rs_b(w)
+
+    for cp in dos:
+        cp.wait_recv()
+    left(kv_y)
+
+    @pl.when(h == 0)
+    def _():
+        for cp in kv_x + kv_d:
+            cp.wait_send()
+
+    lane128 = lax.broadcasted_iota(jnp.int32, (256, 128), 1)
+
+    def prep(zt, _):
+        do = pltpu.roll(DOr[zt].reshape(256, 256).astype(F32), 32, 1)
+        DOs[zt] = do.astype(BF)
+        agree = jnp.sum(do * O[zt], axis=-1, keepdims=True)
+        both = jnp.where(lane128 == 0, LS[zt], jnp.where(lane128 == 1, agree, 0.0))
+        ST[zt] = jnp.transpose(both)[0:8, :]
+        DQ[zt] = jnp.zeros((256, 256), F32)
+        return 0
+
+    lax.fori_loop(0, 4, prep, 0)
+
+    def key_tile(kh, kz, ky):
+        kt = kh * 8 + kz * 2 + ky
+        base = kt - h * 8 - y
+        zlo = jnp.maximum(lax.div(base + 33, 2) - 16, 0)
+        zhi = jnp.minimum(lax.div(base + 40, 2) - 16, 3) + 1
+        DK[...] = jnp.zeros((256, 256), F32)
+        DV[...] = jnp.zeros((256, 256), F32)
+        kk = KV[kh, kz, ky, :, 0:256]
+        vv = KV[kh, kz, ky, :, 128:384]
+        kpos = kt * 256 + lax.broadcasted_iota(jnp.int32, (256, 1), 0)
+
+        def one(zq, _):
+            q = Q[zq]
+            do = DOs[zq]
+            qpos = (h * 8 + zq * 2 + y) * 256 + lax.broadcasted_iota(jnp.int32, (1, 256), 1)
+            seg = seg_of(qpos)
+            st = ST[zq]
+            s = nt(kk, q) * scale
+            ok = (kpos >= seg) & (kpos <= qpos)
+            p = jnp.where(ok, jnp.exp(jnp.where(ok, s - st[0:1, :], 0.0)), 0.0)
+            dp = nt(vv, do)
+            ds = (p * (dp - st[1:2, :])).astype(BF)
+            DK[...] += nn(ds, q)
+            DV[...] += nn(p.astype(BF), do)
+            DQ[zq] += tn(ds, kk)
+            return 0
+
+        lax.fori_loop(zlo, zhi, one, 0)
+        dk = DK[...] * scale
+        dv = DV[...]
+        KV[kh, kz, ky, :, 0:128] = dk[:, 0:128].astype(BF)
+        KV[kh, kz, ky, :, 128:256] = (dk[:, 128:256] + dv[:, 0:128]).astype(BF)
+        KV[kh, kz, ky, :, 256:384] = dv[:, 128:256].astype(BF)
+
+    dkx, dkd, dky = [], [], []
+    for kz in range(4):
+        dkd.append(desc(KV.at[0, kz, yx], DKVr.at[2, kz], dev(0, z, yx, c)))
+        dkx.append(desc(KV.at[0, kz, y], DKVr.at[1, kz], dev(0, z, y, c)))
+
+    @pl.when(h == 1)
+    def _():
+        for kz in range(4):
+            key_tile(0, kz, yx)
+            dkd[kz].start()
+            key_tile(0, kz, y)
+            dkx[kz].start()
+
+    for w in (2, 1, 0):
+        rs_c(w)
+    for kz in range(4):
+        key_tile(h, kz, yx)
+        dky.append(send(KV.at[h, kz, yx], DKVr.at[0, kz], YP))
+    for w in (2, 1, 0):
+        rs_d(w)
+
+    def own_tile(kz, _):
+        key_tile(h, kz, y)
+        return 0
+
+    lax.fori_loop(0, 4, own_tile, 0)
+    for w in (2, 1, 0):
+        rs_e(w)
+
+    for cp in dky:
+        cp.wait_recv()
+
+    @pl.when(h == 0)
+    def _():
+        for cp in dkx + dkd:
+            cp.wait_recv()
+
+    def join(zt, _):
+        dkv = KV[h, zt, y].astype(F32) + DKVr[0, zt].astype(F32)
+        dkv = jnp.where(h == 0, dkv + (DKVr[1, zt].astype(F32) + DKVr[2, zt].astype(F32)), dkv)
+        dq = pltpu.roll(jnp.where(lane256 < 160, DQ[zt] * scale, 0.0), 64, 1)
+        DKVQ[zt, :, 0:256] = dkv[:, 0:256].astype(BF)
+        DKVQ[zt, :, 256:384] = (dkv[:, 256:384] + dq[:, 0:128]).astype(BF)
+        DKVQ[zt, :, 384:512] = dq[:, 128:256].astype(BF)
+        return 0
+
+    lax.fori_loop(0, 4, join, 0)
+
+    VS[...] = jnp.zeros((128, 512), F32)
+
+    def first_grad(zt, _):
+        d = DKVQ[zt]
+        VS[98:99, :] += jnp.sum(d.astype(F32), axis=0, keepdims=True)
+
+        def u_half(i, cols):
+            u = nt(d, W[i].reshape(640, 512))
+            VR[97:98, cols] += jnp.sum(u, axis=0, keepdims=True)
+            U[zt, :, :, cols] = u.astype(BF).reshape(2, 128, 640)
+
+        halves(u_half)
+
+        def gain(i, _):
+            rows = pl.ds(pl.multiple_of(lax.rem(i, 2) * 64, 64), 64)
+            n, _ = stats(T[zt, lax.div(i, 2), rows].astype(F32))
+            VR[96:97, :] += jnp.sum(U[zt, lax.div(i, 2), rows].astype(F32) * n, axis=0, keepdims=True)
+            return 0
+
+        lax.fori_loop(0, 4, gain, 0)
+        return 0
+
+    us = []
+    for k in range(4):
+        first_grad(zs[k], 0)
+        us.append(send(U.at[zs[k], sib], UR.at[zs[k]], SIB))
+
+    VS[99:100, :] = VS[98:99, :]
+    vst = jnp.transpose(VS[...])
+    vlane = lax.broadcasted_iota(jnp.int32, (160, 128), 1)
+    colb[0:1280, :] = jnp.transpose(VR[...])
+    rows = pl.ds(pl.multiple_of(t * 160, 8), 160)
+    colb[rows, :] += jnp.where(vlane == 98, vst[320:480, :], 0.0) + jnp.where(
+        vlane == 99, vst[160:320, :], 0.0
+    )
+
+    uz = []
+    for k in (1, 2, 3, 0):
+        us[k].wait_recv()
+        zt = zs[k]
+        U[zt, c] = (U[zt, c].astype(F32) + UR[zt].astype(F32)).astype(BF)
+        if k:
+            uz.append(send(U.at[zt, c], UZ.at[k - 1], dev(h, zt, y, c)))
+
+    def head_grad(hh, _):
+        g = tn(
+            H[:, :, pl.ds(pl.multiple_of(hh * 640, 128), 640)].reshape(1024, 640),
+            DKVQ[...].reshape(1024, 512),
+        )
+        DW[hh, :, :, :, 0:384] = g[:, 0:384].astype(BF).reshape(4, 2, 80, 384)
+        last = g[:, 384:512] + colb[pl.ds(pl.multiple_of(hh * 640, 128), 640), :]
+        DW[hh, :, :, :, 384:512] = last.astype(BF).reshape(4, 2, 80, 128)
+        return 0
+
+    lax.fori_loop(0, 2, head_grad, 0)
+    dwp = [send(DW.at[ph, :, py], DWr.at[i], d) for i, (ph, py, d) in enumerate(plane)]
+    for cp in dwp:
+        cp.wait_recv()
+    left(wz)
+    for k in range(4):
+        DWz[k] = (
+            DW[h, k, y].astype(F32) + DWr[0, k].astype(F32) + DWr[1, k].astype(F32) + DWr[2, k].astype(F32)
+        ).astype(BF)
+    dwz = [send(DWz.at[zs[k]], DWh.at[z], dev(h, zs[k], y, c)) for k in range(1, 4)]
+    DWh[z] = DWz[z]
+
+    for cp in uz:
+        cp.wait_recv()
+
+    def last_rows(i, _):
+        rows = pl.ds(pl.multiple_of(i * 32, 32), 32)
+        u = U[z, c, rows].astype(F32)
+        for k in range(3):
+            u += UZ[k, rows].astype(F32)
+        n, r = stats(tok[rows, :].astype(F32))
+        wv = u * vec[0:1, :]
+        gt = MID[rows, :] + r * (
+            wv - jnp.mean(wv, axis=-1, keepdims=True) - n * jnp.mean(wv * n, axis=-1, keepdims=True)
+        )
+        gtok_out[rows, :] = gt.astype(BF)
+        return 0
+
+    lax.fori_loop(0, 4, last_rows, 0)
+
+    for cp in dwz:
+        cp.wait_recv()
+    for k in range(4):
+        wasm[k] = DWh[k].astype(F32)
+    wr[...] = wasm[:, pl.ds(pl.multiple_of(sib * 40, 8), 40), :]
+    wo = send(wr, WOr, SIB)
+    wout[c] = wasm[:, pl.ds(pl.multiple_of(c * 40, 8), 40), :]
+    for w in (2, 1, 0):
+        rs_f(w)
+    wo.wait_recv()
+    wout[sib] = WOr[...]
+
+    for cp in pending:
+        cp.wait_send()
+
+    @pl.when(h == 1)
+    def _():
+        for cp in dkx + dkd:
+            cp.wait_send()
+
+    assert count[0] <= NSEM, count[0]
+
+
+NSEM = 192
+
+
+def fast_local(
+    tokens, cotangent, permutation, seq_lengths, first_gain, first_bias, query_weight, query_bias,
+    key_weight, value_weight, value_bias, output_weight, output_bias, second_gain, second_bias,
+    expand_weight, expand_bias, contract_weight, contract_bias,
+):
+    b = lax.axis_index("blk")
+    perm2 = lax.dynamic_index_in_dim(permutation.reshape(2, 16, 128), b, 1, keepdims=False)
+    vectors = [first_gain, first_bias, query_bias, value_bias, output_bias, second_gain, second_bias,
+               expand_bias, contract_bias]
+    vcol = jnp.stack(vectors, axis=1)
+    vcol = jnp.pad(vcol, ((0, 0), (0, 23)))
+    wpre = jnp.concatenate(
+        [key_weight.reshape(40, 8, 160), value_weight.reshape(40, 8, 160), query_weight.reshape(40, 8, 160),
+         jnp.broadcast_to(vcol[:, None, :], (40, 8, 32))], axis=2,
+    )
+    wpre = wpre.reshape(40, 4, 2, 512).transpose(2, 1, 0, 3).astype(F32)
+    fpre = jnp.stack([output_weight, expand_weight, contract_weight]).reshape(3, 40, 2, 640)
+    fpre = fpre.transpose(2, 0, 1, 3).astype(F32)
+
+    vm = pltpu.VMEM
+    fshape = (2, 2, 4, 2, 80, 640)
+    scratch = dict(
+        T=vm((4, 2, 128, 1280), BF), H=vm((4, 256, 1280), BF), W=vm((2, 4, 2, 80, 512), BF),
+        KV=vm((2, 4, 2, 256, 384), BF), Q=vm((4, 256, 256), BF), O=vm((4, 256, 256), F32),
+        F=vm((3,) + fshape, BF), G=vm(fshape, BF), R0=vm((3, 2, 4, 2, 80, 640), BF),
+        R1=vm((3, 2, 4, 80, 640), BF), R2=vm((3, 4, 80, 640), BF), R3=vm((3, 3, 80, 640), BF),
+        FA=vm((3, 80, 640), F32), FR=vm((3, 40, 640), F32),
+        wr=vm((4, 40, 512), F32), wasm=vm((4, 80, 512), F32),
+        fr=vm((3, 40, 640), F32),
+        colb=vm((1408, 128), F32), vec=vm((16, 1280), F32), bias=vm((8, 512), F32),
+        LS=vm((4, 256, 128), F32), ST=vm((4, 8, 256), F32),
+        A=vm((8, 128, 256), BF), As=vm((4, 2, 128, 256), BF), C=vm((2, 128, 1280), BF),
+        RES=vm((2, 128, 1280), BF), MID=vm((128, 1280), F32), N2=vm((128, 1280), F32), RR=vm((128, 128), F32),
+        EX=vm((128, 1280), F32), H2=vm((128, 1280), BF), ACT=vm((128, 1280), BF),
+        CI=vm((128, 1280), BF), DE=vm((128, 1280), BF), GB=vm((128, 1280), BF),
+        DOs=vm((4, 256, 256), BF), DOr=vm((4, 2, 128, 256), BF),
+        DK=vm((256, 256), F32), DV=vm((256, 256), F32), DQ=vm((4, 256, 256), F32),
+        DKVr=vm((3, 4, 256, 384), BF), DKVQ=vm((4, 256, 512), BF), U=vm((4, 2, 128, 1280), BF),
+        UR=vm((4, 128, 1280), BF), UZ=vm((3, 128, 1280), BF), VR=vm((128, 1280), F32),
+        VS=vm((128, 512), F32), DW=vm((2, 4, 2, 80, 512), BF),
+        DWr=vm((3, 4, 80, 512), BF), DWz=vm((4, 80, 512), BF), DWh=vm((4, 80, 512), BF),
+        WOr=vm((4, 40, 512), F32),
+        ss=pltpu.SemaphoreType.DMA((NSEM,)), rs=pltpu.SemaphoreType.DMA((NSEM,)),
+    )
+    vspec = pl.BlockSpec(memory_space=pltpu.VMEM)
+    mixed, gtok, fout, wout = pl.pallas_call(
+        block_kernel,
+        out_shape=(
+            jax.ShapeDtypeStruct((128, 1280), BF), jax.ShapeDtypeStruct((128, 1280), BF),
+            jax.ShapeDtypeStruct((3, 40, 1280), F32), jax.ShapeDtypeStruct((2, 4, 40, 512), F32),
+        ),
+        in_specs=[vspec, vspec, vspec, pl.BlockSpec(memory_space=pltpu.SMEM), vspec, vspec],
+        out_specs=(vspec,) * 4,
+        scratch_shapes=list(scratch.values()),
+        compiler_params=pltpu.CompilerParams(
+            collective_id=0, has_side_effects=True, vmem_limit_bytes=63 * MB,
+        ),
+        cost_estimate=pl.CostEstimate(flops=12_000_000_000, bytes_accessed=6_000_000, transcendentals=5_000_000),
+        name="block",
+    )(tokens, cotangent, perm2, seq_lengths, wpre, fpre)
+    heads = wout.transpose(2, 1, 0, 3).reshape(40, 8, 512)
+    gk = heads[:, :, 0:160].reshape(40, 1280)
+    gv = heads[:, :, 160:320].reshape(40, 1280)
+    gq = heads[:, :, 320:480].reshape(40, 1280)
+    vg = jnp.sum(heads[:, :, 480:489], axis=1)
+    return (
+        mixed, gtok, vg[:, 0], vg[:, 1], gq, vg[:, 2], gk, gv, vg[:, 3], fout[0], vg[:, 4], vg[:, 5],
+        vg[:, 6], fout[1], vg[:, 7], fout[2], vg[:, 8],
+    )
 
 
 def shifted(array, axis, by):
@@ -108,7 +883,9 @@
     head_count = lax.axis_size("head")
     blk_index = lax.axis_index("blk")
     flat_index = lax.axis_index("head") * blk_count + blk_index
-    ends = jnp.cumsum(seq_lengths)
+    count = seq_lengths.shape[0]
+    before = jnp.arange(count)[None, :] <= jnp.arange(count)[:, None]
+    ends = jnp.sum(jnp.where(before, seq_lengths[None, :], 0), axis=1)
     total = permutation.shape[0]
     numbers = jnp.arange(total, dtype=jnp.int32)
     inverse = jnp.zeros((total,), jnp.int32).at[permutation].set(numbers)
@@ -349,7 +1126,7 @@
 
 def solution(mesh):
     return jax.shard_map(
-        local,
+        fast_local if mesh.shape["head"] == 2 and mesh.shape["blk"] == 16 else local,
         mesh=mesh,
         in_specs=(
             P(("head", "blk"), None),

time: 1530 us -> 313 us (0.20)
  waiting for transfers between devices: 817 us -> 0 us
  Pallas kernels: 0 us -> 293 us
  matrix products: 217 us -> 0 us
  local copies, waits for them, and re-layouts: 179 us -> 15.9 us
  blocking collectives: 140 us -> 0 us
  other arithmetic: 99.1 us -> 2.06 us
  starting transfers between devices: 46.6 us -> 0 us
    reduce_scatter x6 -> x0, waiting for transfers between devices: 371 us -> none  [the longest x1 144 us: local(): lax.psum_scatter(grad_value, ('head', 'blk'), scatter_dimension=0, tiled=...]
    pallas_call x0 -> x1, Pallas kernels: none -> 293 us  [fast_local(): pl.pallas_call(block_kernel, out_shape=(jax.ShapeDtypeStruct((128, 1280),...]
    ppermute x64 -> x0, waiting for transfers between devices: 252 us -> none  [shifted(): lax.ppermute(array, axis, [(i, (i + by) % length) for i in range(length)])]
    dot_general x130 -> x0, matrix products: 217 us -> none  [the longest x16 35.4 us: block_terms(): jnp.einsum('hqk,khd->qhd', score_grad, key_block, preferred_element_type=...]
    all_gather x8 -> x0, waiting for transfers between devices: 173 us -> none  [the longest x1 44.7 us: local(): lax.all_gather(query_weight, ('head', 'blk'), axis=0, tiled=True)]
    gather x37 -> x0, local copies, waits for them, and re-layouts: 60.4 us -> none  [the longest x33 56.8 us: layout_initial(): return jnp.take(permutation, places)]
    unnamed x1 -> x0, blocking collectives: 51 us -> none
    convert_element_type x38 -> x2, other arithmetic: 49.7 us -> 1.95 us  [the longest x1 1.06 us: fast_local(): wpre = wpre.reshape(40, 4, 2, 512).transpose(2, 1, 0, 3).astype(F32)]
  transfers between devices with their start and end apart: 83 -> 0, of which waited for: 73 -> 0; matrix products, arithmetic and copies ran while one was open for 32% -> 0% of each run, Pallas kernels for 0% -> 0%
where the time goes in v1:
time: 313 us; the launch traced here: 312 us
  Pallas kernels  293 us (94%)
  local copies, waits for them, and re-layouts  15.9 us (5%)
    pallas_call x1, Pallas kernels, fast_local(): pl.pallas_call(block_kernel, out_shape=(jax.ShapeDtypeStruct((128, 1280),...  293 us
    unnamed x23, local copies, waits for them, and re-layouts  7.06 us

profile of v1, /device:TPU:0, one launch (start us, length us, event | category | flops | bytes accessed | tf_op | source)
XLA Modules:
  0.0 312.3 jit_solution(9187777788136108400)
XLA Ops:
  0.7 0.7 copy-done
  1.4 0.6 constant_dynamic-slice_fusion
  1.9 1.5 stack.51
  3.6 0.9 copy-done.5
  4.5 0.9 copy-done.6
  5.5 0.9 copy-done.7
  6.3 0.2 concatenate.13
  6.6 0.8 copy-done.8
  7.4 0.2 concatenate.11
  7.7 0.8 copy-done.9
  8.5 0.2 concatenate.12
  8.8 1.1 convert_bitcast_fusion.wpre
  9.8 0.9 convert_bitcast_fusion.1.fpre
  10.7 293.4 %block.1 = (bf16[128,1280]{1,0:T(8,128)(2,1)}, bf16[128,1280]{1,0:T(8,128)(2,1)}, f32[3,40,1280]{2,1,0:T(8,128)}, f32[2,4,40,512]{3,2,1,0:T(8,128)}) custom-call(bf16[128,1280]{1,0:T(8,128)(2,1)} %tok.1, bf16[128,1280]{1,0:T(8,128)(2,1)} %cot.1, s32[2,128]{1,0:T(2,128)} %bitcast.27, s32[8]{0:T(128)} %lens.1, f32[2,4,40,512]{3,2,1,0:T(8,128)} %convert_bitcast_fusion.wpre, ...), custom_call_target="tpu_custom_call" | custom-call | flops 12000000000 | bytes 6000000 | tf_op jit(solution)/shard_map/block/pallas_call | solution.py:758
  304.2 2.0 slice_bitcast_fusion
  306.4 0.9 slice_reduce_fusion.1
  307.2 0.2 fusion
  307.6 0.8 reshape.72
  308.5 0.8 reshape.71
  309.5 0.8 reshape.70
  310.3 0.1 copy-done.3
  310.4 0.7 copy.81
  311.2 0.4 copy-done.2
  311.5 0.7 copy.82
  (29 shorter events, 0.9 us)
Async XLA Ops:
  0.7 0.7 copy-start
  0.7 2.9 copy-start.4
  3.6 0.9 copy-start.5
  4.5 0.9 copy-start.6
  5.4 0.9 copy-start.7
  6.5 0.9 copy-start.8
  7.6 0.9 copy-start.9
  304.2 2.0 copy-start.1
  309.5 1.0 copy-start.3
  310.4 1.1 copy-start.2

commit v2 on v1

--- a/solution.py
+++ b/solution.py
@@ -34,13 +34,13 @@
 
 
 def block_kernel(
-    tok, cot, perm2, lens, wpre, fpre,
-    mixed_out, gtok_out, fout, wout,
-    T, H, W, KV, Q, O, F, G, R0, R1, R2, R3, FA, FR,
+    tok, cot, perm, lens, vcol, wq, wk, wv, wts0, wts1, wts2,
+    mixed_out, gtok_out, gq, gk, gv, fo0, fo1, fo2, vgo,
+    WP, FP, T, H, W, KV, Q, O, F, G, R0, R1, R2, R3, FA, FR,
     wr, wasm, fr, colb, vec, bias,
     LS, ST, A, As, C, RES, MID, N2, RR, EX, H2, ACT, CI, DE, GB, DOs, DOr,
     DK, DV, DQ, DKVr, DKVQ, U, UR, UZ, VR, VS, DW, DWr, DWz, DWh, WOr,
-    ss, rs,
+    ss, rs, lss, lrs,
 ):
     h = lax.axis_index("head")
     b = lax.axis_index("blk")
@@ -67,8 +67,6 @@
     P2 = dev(p2h, z, p2y, c)
     XP = dev(hx, z, y, c)
     YP = dev(h, z, yx, c)
-    DP = dev(hx, z, yx, c)
-    plane = [(h, yx, YP), (hx, y, XP), (hx, yx, DP)]
 
     count = [0]
 
@@ -94,46 +92,132 @@
         keep = [cp for cp in pending if not any(cp is one for one in cps)]
         pending[:] = keep
 
+    fout = (fo0, fo1, fo2)
+    for e in range(8):
+        for i, src in enumerate((wk, wv, wq)):
+            WP[e % 2, e // 2, :, i * 160:(i + 1) * 160] = src[:, e * 160:(e + 1) * 160].astype(F32)
+        WP[e % 2, e // 2, :, 480:512] = vcol[...]
+    for w, src in enumerate((wts0, wts1, wts2)):
+        for half in range(2):
+            FP[half, w] = src[:, half * 640:(half + 1) * 640].astype(F32)
+
     bar = pltpu.get_barrier_semaphore()
     for k in range(1, 4):
         pl.semaphore_signal(bar, inc=1, device_id=dev(h, zs[k], y, c), device_id_type=MESH)
         pl.semaphore_signal(bar, inc=1, device_id=dev(h, zs[k], y, sib), device_id_type=MESH)
-    for peer in (SIB, XP, YP, DP):
+    for peer in (SIB, XP, YP):
         pl.semaphore_signal(bar, inc=1, device_id=peer, device_id_type=MESH)
-    pl.semaphore_wait(bar, 10)
-
-    wa = send(wpre.at[sib], wr, SIB)
-    fa = send(fpre.at[sib], fr, SIB)
-    tz = [send(tok, T.at[z, c], dev(h, zs[k], y, c)) for k in range(1, 4)]
-    ts = [send(tok, T.at[z, c], SIB)]
-    cx = send(cot, C.at[h], XP)
+    pl.semaphore_wait(bar, 9)
+
+    up, down = z < 3, z > 0
+    UP = dev(h, jnp.minimum(z + 1, 3), y, c)
+    DOWN = dev(h, jnp.maximum(z - 1, 0), y, c)
+    order = [
+        z,
+        jnp.where(z == 0, 1, jnp.where(z == 3, 2, jnp.where(z == 1, 0, 3))),
+        jnp.where(z == 0, 2, jnp.where(z == 3, 1, jnp.where(z == 1, 2, 1))),
+        jnp.where(z == 0, 3, jnp.where(z == 3, 0, jnp.where(z == 1, 3, 0))),
+    ]
+
+    def tcopy(src, zt, si, device):
+        return pltpu.make_async_remote_copy(
+            src_ref=src, dst_ref=T.at[zt, c], send_sem=lss.at[si], recv_sem=lrs.at[zt],
+            device_id=device, device_id_type=MESH,
+        )
+
+    ts = []
+
+    def token_start():
+        pl.when(up)(tcopy(tok, z, 0, UP).start)
+        pl.when(down)(tcopy(tok, z, 1, DOWN).start)
+        ts.append(send(tok, T.at[z, c], SIB))
+
+    def token_step(k):
+        zt = order[k]
+        here = T.at[zt, c]
+        tcopy(here, zt, 0, UP).wait_recv()
+        pl.when((zt < z) & up)(tcopy(here, zt, 1 + k, UP).start)
+        pl.when((zt > z) & down)(tcopy(here, zt, 1 + k, DOWN).start)
+        ts.append(send(here, here, SIB))
+
+    def token_end():
+        pl.when(up)(tcopy(tok, z, 0, UP).wait_send)
+        pl.when(down)(tcopy(tok, z, 1, DOWN).wait_send)
+        for k in range(1, 4):
+            zt = order[k]
+            here = T.at[zt, c]
+            pl.when((zt < z) & up)(tcopy(here, zt, 1 + k, UP).wait_send)
+            pl.when((zt > z) & down)(tcopy(here, zt, 1 + k, DOWN).wait_send)
+
+    wa = send(WP.at[sib], wr, SIB)
+    fa = send(FP.at[sib], fr, SIB)
     T[z, c] = tok[...]
     C[h] = cot[...]
 
     wa.wait_recv()
-    wasm[:, pl.ds(pl.multiple_of(c * 40, 8), 40), :] = wpre[c]
+    wasm[:, pl.ds(pl.multiple_of(c * 40, 8), 40), :] = WP[c]
     wasm[:, pl.ds(pl.multiple_of(sib * 40, 8), 40), :] = wr[...]
     for k in range(4):
         DWz[k] = wasm[k].astype(BF)
     W[h, z, y] = DWz[z]
     wz = [send(DWz.at[zs[k]], W.at[h, z, y], dev(h, zs[k], y, c)) for k in range(1, 4)]
+    cx = send(cot, C.at[h], XP)
     fa.wait_recv()
-    FA[:, pl.ds(pl.multiple_of(c * 40, 8), 40), :] = fpre[c]
+    FA[:, pl.ds(pl.multiple_of(c * 40, 8), 40), :] = FP[c]
     FA[:, pl.ds(pl.multiple_of(sib * 40, 8), 40), :] = fr[...]
     for w in range(3):
         F[w, c, h, z, y] = FA[w].astype(BF)
+
+    fz = [None] * 3
+
+    def f_line(w):
+        own = F.at[w, c, h, z, y]
+        fz[w] = [send(own, own, dev(h, zs[k], y, c)) for k in range(1, 4)]
+
+    f1, f2a, f2b, fs = [None] * 3, [None] * 3, [None] * 3, []
+
+    def f_plane(w):
+        for cp in fz[w]:
+            cp.wait_recv()
+        own = F.at[w, c, h, :, y]
+        f1[w] = send(own, own, P1)
+        f2a[w] = send(own, own, P2)
+        one = send(own, own, SIB)
+        fs.append(one)
+        fs_w[id(one)] = w
+
+    def f_forward(w):
+        f1[w].wait_recv()
+        got = F.at[w, c, p1h, :, p1y]
+        f2b[w] = send(got, got, P2)
+        one = send(got, got, SIB)
+        fs.append(one)
+        fs_w[id(one)] = w
+
+    flast = [None] * 3
+    fs_w = {}
+
+    def f_last(w):
+        f2a[w].wait_recv()
+        got = F.at[w, c, p2h, :, p2y]
+        one = send(got, got, SIB)
+        f2b[w].wait_recv()
+        got = F.at[w, c, hx, :, yx]
+        flast[w] = [one, send(got, got, SIB)]
+
+    f_line(0)
+    token_start()
     for cp in wz:
         cp.wait_recv()
-    wp = [send(W.at[h, :, y], W.at[h, :, y], d) for (_, _, d) in plane]
-    fz = [
-        [send(F.at[w, c, h, z, y], F.at[w, c, h, z, y], dev(h, zs[k], y, c)) for k in range(1, 4)]
-        for w in range(3)
-    ]
-    for k in range(1, 4):
-        tz[k - 1].wait_recv()
-        ts.append(send(T.at[zr[k], c], T.at[zr[k], c], SIB))
-    for cp in wp:
-        cp.wait_recv()
+    own = W.at[h, :, y]
+    w1 = send(own, own, P1)
+    w2 = send(own, own, P2)
+    w1.wait_recv()
+    got = W.at[p1h, :, p1y]
+    w3 = send(got, got, P2)
+    f_plane(0)
+    w2.wait_recv()
+    w3.wait_recv()
 
     def tcol(hh, _):
         colb[pl.ds(pl.multiple_of(hh * 640, 128), 640), :] = (
@@ -151,9 +235,10 @@
 
     lane256 = lax.broadcasted_iota(jnp.int32, (256, 256), 1)
 
-    kv_y, kv_x, kv_d = [], [], []
-    for k in range(4):
-        zt = zr[k]
+    kv1, kv2, kv3 = [], [], []
+
+    def project(k):
+        zt = order[k]
         ts[k].wait_recv()
 
         def norm(i, _):
@@ -168,40 +253,31 @@
         qr = pltpu.roll(kvq[:, 256:512], 192, 1)
         Q[zt] = jnp.where(lane256 < 160, qr, 0.0).astype(BF)
         src = KV.at[h, zt, y]
-        kv_y.append(send(src, KV.at[h, zt, y], YP))
-        cpx = desc(src, KV.at[h, zt, y], XP)
-        cpd = desc(src, KV.at[h, zt, y], DP)
-        kv_x.append(cpx)
-        kv_d.append(cpd)
-
-        @pl.when(h == 0)
-        def _():
-            cpx.start()
-            cpd.start()
-
-    f1, f2a, fs = [], [], []
-    for w in range(3):
-        for cp in fz[w]:
-            cp.wait_recv()
-        own = F.at[w, c, h, :, y]
-        f1.append(send(own, own, P1))
-        f2a.append(send(own, own, P2))
-        fs.append(send(own, own, SIB))
-
-    for cp in kv_y:
+        kv1.append(send(src, src, P1))
+        kv2.append(send(src, src, P2))
+
+    def kv_forward(k):
+        kv1[k].wait_recv()
+        got = KV.at[p1h, order[k], p1y]
+        kv3.append(send(got, got, P2))
+
+    project(0)
+    token_step(1)
+    f_forward(0)
+    project(1)
+    kv_forward(0)
+    token_step(2)
+    project(2)
+    kv_forward(1)
+    token_step(3)
+    f_line(1)
+    project(3)
+    kv_forward(2)
+    kv_forward(3)
+    f_line(2)
+    f_plane(1)
+    for cp in kv2 + kv3:
         cp.wait_recv()
-
-    @pl.when(h == 1)
-    def _():
-        for cp in kv_x + kv_d:
-            cp.wait_recv()
-
-    f2b = []
-    for w in range(3):
-        f1[w].wait_recv()
-        got = F.at[w, c, p1h, :, p1y]
-        f2b.append(send(got, got, P2))
-        fs.append(send(got, got, SIB))
 
     scale = HEAD_DIM ** -0.5
     ends = []
@@ -259,19 +335,25 @@
             if k == 0 and cc is c:
                 continue
             asend.append(send(As.at[zt, cc], A.at[t], dev(h, zt, y, cc)))
+        if k == 1:
+            f_plane(2)
+        if k == 2:
+            f_forward(1)
+        if k == 3:
+            f_forward(2)
     A[t] = As[z, c]
 
-    for w in range(3):
-        f2a[w].wait_recv()
-        got = F.at[w, c, p2h, :, p2y]
-        fs.append(send(got, got, SIB))
-        f2b[w].wait_recv()
-        got = F.at[w, c, hx, :, yx]
-        fs.append(send(got, got, SIB))
+    f_last(0)
     for cp in asend:
         cp.wait_recv()
-    for cp in fs:
-        cp.wait_recv()
+
+    def f_done(w):
+        for cp in flast[w] + fs[2 * w:2 * w + 2]:
+            cp.wait_recv()
+
+    fs.sort(key=lambda cp: fs_w[id(cp)])
+    f_done(0)
+    f_last(1)
 
     VR[...] = jnp.zeros((128, 1280), F32)
 
@@ -306,20 +388,16 @@
         ACT[:, cols] = (ex * phi).astype(BF)
         EX[:, cols] = phi + ex * jnp.exp(-0.5 * ex * ex) * 0.3989422804014327
 
+    f_done(1)
+    f_last(2)
     halves(exp_half)
-
-    def con_half(i, cols):
-        res = MID[:, cols] + nn(ACT[...], F[2, i].reshape(1280, 640)) + vec[8:9, cols]
-        RES[h, :, cols] = res.astype(BF)
-
-    halves(con_half)
-    rx = send(RES.at[h], RES.at[h], XP)
 
     cx.wait_recv()
     i_sub = lax.broadcasted_iota(jnp.int32, (128, 128), 0)
     mine0 = (h * 16 + b) * 128
-    oh0 = jnp.where(perm2[0:1, :] == mine0 + i_sub, 1.0, 0.0).astype(BF)
-    oh1 = jnp.where(perm2[1:2, :] == mine0 + i_sub, 1.0, 0.0).astype(BF)
+    pr0, pr1 = perm[pl.ds(b, 1), :], perm[pl.ds(16 + b, 1), :]
+    oh0 = jnp.where(pr0 == mine0 + i_sub, 1.0, 0.0).astype(BF)
+    oh1 = jnp.where(pr1 == mine0 + i_sub, 1.0, 0.0).astype(BF)
 
     def cot_half(i, cols):
         ci = nn(oh0, C[0, :, cols]) + nn(oh1, C[1, :, cols])
@@ -327,15 +405,6 @@
         VR[104:105, cols] = jnp.sum(ci, axis=0, keepdims=True)
 
     halves(cot_half)
-
-    def act_half(i, cols):
-        f0, f1w = F[2, 0, i].reshape(640, 640), F[2, 1, i].reshape(640, 640)
-        dact = nt(CI[:, 0:640], f0) + nt(CI[:, 640:1280], f1w)
-        de = (dact * EX[:, cols]).astype(BF)
-        DE[:, cols] = de
-        VR[103:104, cols] = jnp.sum(de.astype(F32), axis=0, keepdims=True)
-
-    halves(act_half)
 
     def outer(left, right, dst):
         def one(i, _):
@@ -355,13 +424,90 @@
     def rs_a(w):
         ra[w] = send(Gw[w].at[sib], R0.at[w], SIB)
 
+    r1, r2s, r3, r4 = [None] * 3, [None] * 3, [None] * 3, [None] * 3
+
+    def rs_b(w):
+        ra[w].wait_recv()
+        gw = Gw[w]
+
+        def one(i, _):
+            ih, iz = lax.div(i, 4), lax.rem(i, 4)
+            gw[c, ih, iz] = (gw[c, ih, iz].astype(F32) + R0[w, ih, iz].astype(F32)).astype(BF)
+            return 0
+
+        lax.fori_loop(0, 8, one, 0)
+        r1[w] = [
+            send(gw.at[c, hx, :, yx], R1.at[w, 1], P2),
+            send(gw.at[c, p2h, :, p2y], R1.at[w, 0], P2),
+        ]
+
+    def rs_c(w):
+        gw = Gw[w]
+        for cp in r1[w]:
+            cp.wait_recv()
+
+        def one(i, _):
+            gw[c, p1h, i, p1y] = (gw[c, p1h, i, p1y].astype(F32) + R1[w, 1, i].astype(F32)).astype(BF)
+            return 0
+
+        lax.fori_loop(0, 4, one, 0)
+        r2s[w] = send(gw.at[c, p1h, :, p1y], R2.at[w], P1)
+
+    def rs_d(w):
+        gw = Gw[w]
+        r2s[w].wait_recv()
+
+        def two(i, _):
+            gw[c, h, i, y] = (
+                gw[c, h, i, y].astype(F32) + R1[w, 0, i].astype(F32) + R2[w, i].astype(F32)
+            ).astype(BF)
+            return 0
+
+        lax.fori_loop(0, 4, two, 0)
+        r3[w] = [send(gw.at[c, h, zs[k], y], R3.at[w, k - 1], dev(h, zs[k], y, c)) for k in range(1, 4)]
+
+    def rs_e(w):
+        gw = Gw[w]
+        total = gw[c, h, z, y].astype(F32)
+        for k in range(1, 4):
+            r3[w][k - 1].wait_recv()
+            total += R3[w, k - 1].astype(F32)
+        FA[w] = total
+        r4[w] = send(FA.at[w, pl.ds(pl.multiple_of(sib * 40, 8), 40)], FR.at[w], SIB)
+
+    def rs_f(w):
+        r4[w].wait_recv()
+        fout[w][:, pl.ds(pl.multiple_of(c * 640, 128), 640)] = FA[w, pl.ds(pl.multiple_of(c * 40, 8), 40)]
+        fout[w][:, pl.ds(pl.multiple_of(sib * 640, 128), 640)] = FR[w]
+
     outer(ACT, CI, G)
     rs_a(2)
+    f_done(2)
+    def con_half(i, cols):
+        res = MID[:, cols] + nn(ACT[...], F[2, i].reshape(1280, 640)) + vec[8:9, cols]
+        RES[h, :, cols] = res.astype(BF)
+
+    halves(con_half)
+    rx = send(RES.at[h], RES.at[h], XP)
+
+    def act_half(i, cols):
+        f0, f1w = F[2, 0, i].reshape(640, 640), F[2, 1, i].reshape(640, 640)
+        dact = nt(CI[:, 0:640], f0) + nt(CI[:, 640:1280], f1w)
+        de = (dact * EX[:, cols]).astype(BF)
+        DE[:, cols] = de
+        VR[103:104, cols] = jnp.sum(de.astype(F32), axis=0, keepdims=True)
+
+    halves(act_half)
+    left([cp for row in fz + flast for cp in row] + f1 + f2a + f2b + fs)
+    outer(H2, DE, F.at[2])
+    rs_a(1)
+
 
     def back_half(i, cols):
         f0, f1w = F[1, 0, i].reshape(640, 640), F[1, 1, i].reshape(640, 640)
         EX[:, cols] = nt(DE[:, 0:640], f0) + nt(DE[:, 640:1280], f1w)
 
+    rs_b(2)
     halves(back_half)
 
     def norm2_back(i, _):
@@ -400,9 +546,6 @@
             dos.append(send(As.at[zs[k], cc], DOr.at[z, c], dev(h, zs[k], y, cc)))
     DOr[z, c] = As[z, c]
 
-    left([cp for row in fz for cp in row] + f1 + f2a + f2b + fs)
-    outer(H2, DE, F.at[2])
-    rs_a(1)
 
     def outo(e, _):
         def one(half, _):
@@ -413,11 +556,12 @@
         lax.fori_loop(0, 2, one, 0)
         return 0
 
+    rs_b(1)
     lax.fori_loop(0, 8, outo, 0)
     rs_a(0)
 
     rx.wait_recv()
-    pm = jnp.where(h == 0, perm2[0:1, :], perm2[1:2, :])
+    pm = perm[pl.ds(h * 16 + b, 1), :]
     om0 = jnp.where(pm == b * 128 + i_sub, 1.0, 0.0).astype(BF)
     om1 = jnp.where(pm == (16 + b) * 128 + i_sub, 1.0, 0.0).astype(BF)
 
@@ -425,85 +569,12 @@
         mixed_out[:, cols] = (tn(om0, RES[0, :, cols]) + tn(om1, RES[1, :, cols])).astype(BF)
 
     halves(mix_half)
-
-    def add_into(dst_at, others):
-        def one(i, _):
-            ref, idx = dst_at(i)
-            total = ref[idx].astype(F32)
-            for other in others:
-                total += other(i).astype(F32)
-            ref[idx] = total.astype(BF)
-            return 0
-
-        return one
-
-    r1, r2s, r3, r4 = [None] * 3, [None] * 3, [None] * 3, [None] * 3
-
-    def rs_b(w):
-        ra[w].wait_recv()
-        gw = Gw[w]
-
-        def one(i, _):
-            ih, iz = lax.div(i, 4), lax.rem(i, 4)
-            gw[c, ih, iz] = (gw[c, ih, iz].astype(F32) + R0[w, ih, iz].astype(F32)).astype(BF)
-            return 0
-
-        lax.fori_loop(0, 8, one, 0)
-        r1[w] = [
-            send(gw.at[c, hx, :, yx], R1.at[w, 1], P2),
-            send(gw.at[c, p2h, :, p2y], R1.at[w, 0], P2),
-        ]
-
-    def rs_c(w):
-        gw = Gw[w]
-        for cp in r1[w]:
-            cp.wait_recv()
-
-        def one(i, _):
-            gw[c, p1h, i, p1y] = (gw[c, p1h, i, p1y].astype(F32) + R1[w, 1, i].astype(F32)).astype(BF)
-            return 0
-
-        lax.fori_loop(0, 4, one, 0)
-        r2s[w] = send(gw.at[c, p1h, :, p1y], R2.at[w], P1)
-
-    def rs_d(w):
-        gw = Gw[w]
-        r2s[w].wait_recv()
-
-        def two(i, _):
-            gw[c, h, i, y] = (
-                gw[c, h, i, y].astype(F32) + R1[w, 0, i].astype(F32) + R2[w, i].astype(F32)
-            ).astype(BF)
-            return 0
-
-        lax.fori_loop(0, 4, two, 0)
-        r3[w] = [send(gw.at[c, h, zs[k], y], R3.at[w, k - 1], dev(h, zs[k], y, c)) for k in range(1, 4)]
-
-    def rs_e(w):
-        gw = Gw[w]
-        total = gw[c, h, z, y].astype(F32)
-        for k in range(1, 4):
-            r3[w][k - 1].wait_recv()
-            total += R3[w, k - 1].astype(F32)
-        FA[w] = total
-        r4[w] = send(FA.at[w, pl.ds(pl.multiple_of(sib * 40, 8), 40)], FR.at[w], SIB)
-
-    def rs_f(w):
-        r4[w].wait_recv()
-        fout[w, :, pl.ds(pl.multiple_of(c * 640, 128), 640)] = FA[w, pl.ds(pl.multiple_of(c * 40, 8), 40)]
-        fout[w, :, pl.ds(pl.multiple_of(sib * 640, 128), 640)] = FR[w]
-
-    for w in (2, 1, 0):
-        rs_b(w)
+    rs_b(0)
+
 
     for cp in dos:
         cp.wait_recv()
-    left(kv_y)
-
-    @pl.when(h == 0)
-    def _():
-        for cp in kv_x + kv_d:
-            cp.wait_send()
+    left(kv1 + kv2 + kv3)
 
     lane128 = lax.broadcasted_iota(jnp.int32, (256, 128), 1)
 
@@ -552,53 +623,41 @@
         KV[kh, kz, ky, :, 128:256] = (dk[:, 128:256] + dv[:, 0:128]).astype(BF)
         KV[kh, kz, ky, :, 256:384] = dv[:, 128:256].astype(BF)
 
-    dkx, dkd, dky = [], [], []
-    for kz in range(4):
-        dkd.append(desc(KV.at[0, kz, yx], DKVr.at[2, kz], dev(0, z, yx, c)))
-        dkx.append(desc(KV.at[0, kz, y], DKVr.at[1, kz], dev(0, z, y, c)))
-
-    @pl.when(h == 1)
-    def _():
-        for kz in range(4):
-            key_tile(0, kz, yx)
-            dkd[kz].start()
-            key_tile(0, kz, y)
-            dkx[kz].start()
-
-    for w in (2, 1, 0):
-        rs_c(w)
-    for kz in range(4):
-        key_tile(h, kz, yx)
-        dky.append(send(KV.at[h, kz, yx], DKVr.at[0, kz], YP))
-    for w in (2, 1, 0):
-        rs_d(w)
+    dk0, dk1, dk2 = {}, {}, {}
+    turn = (1, 2, 3, 0)
+    for k in turn:
+        kz = zs[k]
+        key_tile(hx, kz, yx)
+        dk1[k] = send(KV.at[hx, kz, yx], DKVr.at[1, kz], P2)
+        key_tile(p2h, kz, p2y)
+        dk0[k] = send(KV.at[p2h, kz, p2y], DKVr.at[0, kz], P2)
+    rs_c(2)
+    for k in turn:
+        kz = zs[k]
+        key_tile(p1h, kz, p1y)
+        dk1[k].wait_recv()
+        KV[p1h, kz, p1y] = (KV[p1h, kz, p1y].astype(F32) + DKVr[1, kz].astype(F32)).astype(BF)
+        dk2[k] = send(KV.at[p1h, kz, p1y], DKVr.at[2, kz], P1)
+    rs_d(2)
+    rs_c(1)
 
     def own_tile(kz, _):
         key_tile(h, kz, y)
         return 0
 
     lax.fori_loop(0, 4, own_tile, 0)
-    for w in (2, 1, 0):
-        rs_e(w)
-
-    for cp in dky:
-        cp.wait_recv()
-
-    @pl.when(h == 0)
-    def _():
-        for cp in dkx + dkd:
-            cp.wait_recv()
+    rs_c(0)
+    rs_e(2)
+    rs_d(1)
 
     def join(zt, _):
-        dkv = KV[h, zt, y].astype(F32) + DKVr[0, zt].astype(F32)
-        dkv = jnp.where(h == 0, dkv + (DKVr[1, zt].astype(F32) + DKVr[2, zt].astype(F32)), dkv)
+        dkv = KV[h, zt, y].astype(F32) + DKVr[0, zt].astype(F32) + DKVr[2, zt].astype(F32)
         dq = pltpu.roll(jnp.where(lane256 < 160, DQ[zt] * scale, 0.0), 64, 1)
         DKVQ[zt, :, 0:256] = dkv[:, 0:256].astype(BF)
         DKVQ[zt, :, 256:384] = (dkv[:, 256:384] + dq[:, 0:128]).astype(BF)
         DKVQ[zt, :, 384:512] = dq[:, 128:256].astype(BF)
         return 0
 
-    lax.fori_loop(0, 4, join, 0)
 
     VS[...] = jnp.zeros((128, 512), F32)
 
@@ -623,10 +682,14 @@
         return 0
 
     us = []
-    for k in range(4):
+    for k in turn:
+        dk0[k].wait_recv()
+        dk2[k].wait_recv()
+        join(zs[k], 0)
         first_grad(zs[k], 0)
         us.append(send(U.at[zs[k], sib], UR.at[zs[k]], SIB))
 
+    rs_d(0)
     VS[99:100, :] = VS[98:99, :]
     vst = jnp.transpose(VS[...])
     vlane = lax.broadcasted_iota(jnp.int32, (160, 128), 1)
@@ -637,8 +700,8 @@
     )
 
     uz = []
-    for k in (1, 2, 3, 0):
-        us[k].wait_recv()
+    for i, k in enumerate((1, 2, 3, 0)):
+        us[i].wait_recv()
         zt = zs[k]
         U[zt, c] = (U[zt, c].astype(F32) + UR[zt].astype(F32)).astype(BF)
         if k:
@@ -655,13 +718,19 @@
         return 0
 
     lax.fori_loop(0, 2, head_grad, 0)
-    dwp = [send(DW.at[ph, :, py], DWr.at[i], d) for i, (ph, py, d) in enumerate(plane)]
-    for cp in dwp:
-        cp.wait_recv()
+    dw1 = send(DW.at[hx, :, yx], DWr.at[1], P2)
+    rs_e(1)
+    rs_e(0)
+    dw0 = send(DW.at[p2h, :, p2y], DWr.at[0], P2)
+    dw1.wait_recv()
+    DW[p1h, :, p1y] = (DW[p1h, :, p1y].astype(F32) + DWr[1].astype(F32)).astype(BF)
+    dw2 = send(DW.at[p1h, :, p1y], DWr.at[2], P1)
+    dw0.wait_recv()
+    dw2.wait_recv()
     left(wz)
     for k in range(4):
         DWz[k] = (
-            DW[h, k, y].astype(F32) + DWr[0, k].astype(F32) + DWr[1, k].astype(F32) + DWr[2, k].astype(F32)
+            DW[h, k, y].astype(F32) + DWr[0, k].astype(F32) + DWr[2, k].astype(F32)
         ).astype(BF)
     dwz = [send(DWz.at[zs[k]], DWh.at[z], dev(h, zs[k], y, c)) for k in range(1, 4)]
     DWh[z] = DWz[z]
@@ -690,24 +759,38 @@
         wasm[k] = DWh[k].astype(F32)
     wr[...] = wasm[:, pl.ds(pl.multiple_of(sib * 40, 8), 40), :]
     wo = send(wr, WOr, SIB)
-    wout[c] = wasm[:, pl.ds(pl.multiple_of(c * 40, 8), 40), :]
+    left([wa])
+    WP[c] = wasm[:, pl.ds(pl.multiple_of(c * 40, 8), 40), :]
     for w in (2, 1, 0):
         rs_f(w)
     wo.wait_recv()
-    wout[sib] = WOr[...]
-
+    WP[sib] = WOr[...]
+    total = jnp.zeros((40, 128), F32)
+    for e in range(8):
+        for i, dst in enumerate((gk, gv, gq)):
+            dst[:, e * 160:(e + 1) * 160] = WP[e % 2, e // 2, :, i * 160:(i + 1) * 160]
+        total += WP[e % 2, e // 2, :, 384:512]
+    colb[0:40, :] = total
+    vgo[...] = jnp.transpose(colb[0:128, :])[96:112, :]
+
+    token_end()
     for cp in pending:
         cp.wait_send()
 
-    @pl.when(h == 1)
-    def _():
-        for cp in dkx + dkd:
-            cp.wait_send()
-
     assert count[0] <= NSEM, count[0]
 
 
 NSEM = 192
+
+
+def hand_over(*refs):
+    n = len(refs) // 2
+    sems = refs[-1]
+    copies = [pltpu.make_async_copy(refs[i], refs[n + i], sems.at[i]) for i in range(n)]
+    for cp in copies:
+        cp.start()
+    for cp in copies:
+        cp.wait()
 
 
 def fast_local(
@@ -715,23 +798,15 @@
     key_weight, value_weight, value_bias, output_weight, output_bias, second_gain, second_bias,
     expand_weight, expand_bias, contract_weight, contract_bias,
 ):
-    b = lax.axis_index("blk")
-    perm2 = lax.dynamic_index_in_dim(permutation.reshape(2, 16, 128), b, 1, keepdims=False)
     vectors = [first_gain, first_bias, query_bias, value_bias, output_bias, second_gain, second_bias,
                expand_bias, contract_bias]
-    vcol = jnp.stack(vectors, axis=1)
-    vcol = jnp.pad(vcol, ((0, 0), (0, 23)))
-    wpre = jnp.concatenate(
-        [key_weight.reshape(40, 8, 160), value_weight.reshape(40, 8, 160), query_weight.reshape(40, 8, 160),
-         jnp.broadcast_to(vcol[:, None, :], (40, 8, 32))], axis=2,
-    )
-    wpre = wpre.reshape(40, 4, 2, 512).transpose(2, 1, 0, 3).astype(F32)
-    fpre = jnp.stack([output_weight, expand_weight, contract_weight]).reshape(3, 40, 2, 640)
-    fpre = fpre.transpose(2, 0, 1, 3).astype(F32)
+    vcol = jnp.pad(jnp.stack(vectors, axis=1).astype(F32), ((0, 0), (0, 23)))
+    perm = permutation.reshape(32, 128)
 
     vm = pltpu.VMEM
     fshape = (2, 2, 4, 2, 80, 640)
     scratch = dict(
+        WP=vm((2, 4, 40, 512), F32), FP=vm((2, 3, 40, 640), F32),
         T=vm((4, 2, 128, 1280), BF), H=vm((4, 256, 1280), BF), W=vm((2, 4, 2, 80, 512), BF),
         KV=vm((2, 4, 2, 256, 384), BF), Q=vm((4, 256, 256), BF), O=vm((4, 256, 256), F32),
         F=vm((3,) + fshape, BF), G=vm(fshape, BF), R0=vm((3, 2, 4, 2, 80, 640), BF),
@@ -753,32 +828,35 @@
         DWr=vm((3, 4, 80, 512), BF), DWz=vm((4, 80, 512), BF), DWh=vm((4, 80, 512), BF),
         WOr=vm((4, 40, 512), F32),
         ss=pltpu.SemaphoreType.DMA((NSEM,)), rs=pltpu.SemaphoreType.DMA((NSEM,)),
+        lss=pltpu.SemaphoreType.DMA((5,)), lrs=pltpu.SemaphoreType.DMA((4,)),
     )
     vspec = pl.BlockSpec(memory_space=pltpu.VMEM)
-    mixed, gtok, fout, wout = pl.pallas_call(
+    rows = jax.ShapeDtypeStruct((40, 1280), F32)
+    tokens_out = jax.ShapeDtypeStruct((128, 1280), BF)
+    mixed, gtok, gq, gk, gv, go, ge, gc, vg = pl.pallas_call(
         block_kernel,
-        out_shape=(
-            jax.ShapeDtypeStruct((128, 1280), BF), jax.ShapeDtypeStruct((128, 1280), BF),
-            jax.ShapeDtypeStruct((3, 40, 1280), F32), jax.ShapeDtypeStruct((2, 4, 40, 512), F32),
-        ),
-        in_specs=[vspec, vspec, vspec, pl.BlockSpec(memory_space=pltpu.SMEM), vspec, vspec],
-        out_specs=(vspec,) * 4,
+        out_shape=(tokens_out, tokens_out) + (rows,) * 6 + (jax.ShapeDtypeStruct((16, 128), F32),),
+        in_specs=[vspec, vspec, vspec, pl.BlockSpec(memory_space=pltpu.SMEM)] + [vspec] * 7,
+        out_specs=(vspec,) * 9,
         scratch_shapes=list(scratch.values()),
         compiler_params=pltpu.CompilerParams(
             collective_id=0, has_side_effects=True, vmem_limit_bytes=63 * MB,
         ),
         cost_estimate=pl.CostEstimate(flops=12_000_000_000, bytes_accessed=6_000_000, transcendentals=5_000_000),
         name="block",
-    )(tokens, cotangent, perm2, seq_lengths, wpre, fpre)
-    heads = wout.transpose(2, 1, 0, 3).reshape(40, 8, 512)
-    gk = heads[:, :, 0:160].reshape(40, 1280)
-    gv = heads[:, :, 160:320].reshape(40, 1280)
-    gq = heads[:, :, 320:480].reshape(40, 1280)
-    vg = jnp.sum(heads[:, :, 480:489], axis=1)
-    return (
-        mixed, gtok, vg[:, 0], vg[:, 1], gq, vg[:, 2], gk, gv, vg[:, 3], fout[0], vg[:, 4], vg[:, 5],
-        vg[:, 6], fout[1], vg[:, 7], fout[2], vg[:, 8],
-    )
+    )(tokens, cotangent, perm, seq_lengths, vcol, query_weight, key_weight, value_weight, output_weight,
+      expand_weight, contract_weight)
+    any_spec = pl.BlockSpec(memory_space=pl.ANY)
+    mixed, gtok, gq, gk, gv, go, ge, gc = pl.pallas_call(
+        hand_over,
+        out_shape=(tokens_out, tokens_out) + (rows,) * 6,
+        in_specs=[vspec] * 8,
+        out_specs=(any_spec,) * 8,
+        scratch_shapes=[pltpu.SemaphoreType.DMA((8,))],
+        name="hand_over",
+    )(mixed, gtok, gq, gk, gv, go, ge, gc)
+    v = [vg[j, 0:40] for j in range(9)]
+    return mixed, gtok, v[0], v[1], gq, v[2], gk, gv, v[3], go, v[4], v[5], v[6], ge, v[7], gc, v[8]
 
 
 def shifted(array, axis, by):

time: 313 us -> 246 us (0.79)
  Pallas kernels: 293 us -> 243 us
  local copies, waits for them, and re-layouts: 15.9 us -> 2.1 us
    pallas_call x1 -> x2, Pallas kernels: 293 us -> 243 us  [the longest x1 240 us: fast_local(): pl.pallas_call(block_kernel, out_shape=(tokens_out, tokens_out) + (rows,)...]
    unnamed x23 -> x20, local copies, waits for them, and re-layouts: 7.06 us -> 1.4 us
where the time goes in v2:
time: 246 us
  Pallas kernels  243 us (99%)
    pallas_call x1, Pallas kernels, fast_local(): pl.pallas_call(block_kernel, out_shape=(tokens_out, tokens_out) + (rows,)...  240 us

profile of v2, /device:TPU:0, one launch (start us, length us, event | category | flops | bytes accessed | tf_op | source)
XLA Modules:
  0.0 246.3 jit_solution(15438967824010786293)
XLA Ops:
  0.7 0.0 copy-start.8
  0.7 0.0 copy-start.9
  0.7 0.0 copy-start.4
  0.7 0.0 copy-start.5
  0.7 0.0 copy-start.6
  0.7 0.0 copy-start.7
  0.7 0.0 copy-start.1
  0.7 0.6 copy-done.8
  1.3 0.0 copy-done.9
  1.3 0.0 copy-done.4
  1.3 0.0 copy-done.5
  1.4 0.0 copy-done.6
  1.4 0.0 copy-done.7
  1.4 0.0 copy-done.1
  1.4 0.0 copy-done.2
  1.4 0.0 copy-done.3
  1.4 0.1 stack.39
  1.5 0.1 copy.45
  1.6 0.6 pad_convert_fusion.vcol
  2.2 240.0 %block.1 = (bf16[128,1280]{1,0:T(8,128)(2,1)}, bf16[128,1280]{1,0:T(8,128)(2,1)}, f32[40,1280]{1,0:T(8,128)}, f32[40,1280]{1,0:T(8,128)}, f32[40,1280]{1,0:T(8,1...) custom-call(bf16[128,1280]{1,0:T(8,128)(2,1)} %tok.1, ...), custom_call_target="tpu_custom_call" | custom-call | flops 12000000000 | bytes 6000000 | tf_op jit(solution)/shard_map/block/pallas_call | solution.py:836
  242.2 2.8 %hand_over.1 = (bf16[128,1280]{1,0:T(8,128)(2,1)}, bf16[128,1280]{1,0:T(8,128)(2,1)}, f32[40,1280]{1,0:T(8,128)}, f32[40,1280]{1,0:T(8,128)}, f32[40,1280]{1,0:T...) custom-call(bf16[128,1280]{1,0:T(8,128)(2,1)} %get-tuple-element.34.refs_0_, ...), custom_call_target="tpu_custom_call" | custom-call | tf_op jit(solution)/shard_map/hand_over/pallas_call | solution.py:850
  245.0 0.0 copy-start
  245.0 0.7 copy-done
  245.7 0.5 slice_bitcast_fusion
  (2 shorter events, 0.0 us)
Async XLA Ops:
  0.7 0.7 copy-start.8
  0.7 0.7 copy-start.9
  0.7 0.7 copy-start.4
  0.7 0.7 copy-start.5
  0.7 0.7 copy-start.6
  0.7 0.7 copy-start.7
  0.7 0.7 copy-start.1
  0.7 0.7 copy-start.2
  0.7 0.7 copy-start.3
  245.0 0.7 copy-start

commit v3 on v2

--- a/solution.py
+++ b/solution.py
@@ -36,9 +36,9 @@
 def block_kernel(
     tok, cot, perm, lens, vcol, wq, wk, wv, wts0, wts1, wts2,
     mixed_out, gtok_out, gq, gk, gv, fo0, fo1, fo2, vgo,
-    WP, FP, T, H, W, KV, Q, O, F, G, R0, R1, R2, R3, FA, FR,
+    WP, FP, T, H, W, KV, Q, QT, OT, F, G, R0, R1, R2, R3, FA, FR,
     wr, wasm, fr, colb, vec, bias,
-    LS, ST, A, As, C, RES, MID, N2, RR, EX, H2, ACT, CI, DE, GB, DOs, DOr,
+    MS, TS, A, As, C, RES, MID, EX, H2, ACT, CI, DE, GB, DOs, DOT, DOr,
     DK, DV, DQ, DKVr, DKVQ, U, UR, UZ, VR, VS, DW, DWr, DWz, DWh, WOr,
     ss, rs, lss, lrs,
 ):
@@ -92,6 +92,13 @@
         keep = [cp for cp in pending if not any(cp is one for one in cps)]
         pending[:] = keep
 
+    bar = pltpu.get_barrier_semaphore()
+    for k in range(1, 4):
+        pl.semaphore_signal(bar, inc=1, device_id=dev(h, zs[k], y, c), device_id_type=MESH)
+        pl.semaphore_signal(bar, inc=1, device_id=dev(h, zs[k], y, sib), device_id_type=MESH)
+    for peer in (SIB, XP, YP):
+        pl.semaphore_signal(bar, inc=1, device_id=peer, device_id_type=MESH)
+
     fout = (fo0, fo1, fo2)
     for e in range(8):
         for i, src in enumerate((wk, wv, wq)):
@@ -101,12 +108,6 @@
         for half in range(2):
             FP[half, w] = src[:, half * 640:(half + 1) * 640].astype(F32)
 
-    bar = pltpu.get_barrier_semaphore()
-    for k in range(1, 4):
-        pl.semaphore_signal(bar, inc=1, device_id=dev(h, zs[k], y, c), device_id_type=MESH)
-        pl.semaphore_signal(bar, inc=1, device_id=dev(h, zs[k], y, sib), device_id_type=MESH)
-    for peer in (SIB, XP, YP):
-        pl.semaphore_signal(bar, inc=1, device_id=peer, device_id_type=MESH)
     pl.semaphore_wait(bar, 9)
 
     up, down = z < 3, z > 0
@@ -251,7 +252,9 @@
         kvq = nn(H[zt], W[...].reshape(1280, 512)) + bias[0:1, :]
         KV[h, zt, y] = kvq[:, 0:384].astype(BF)
         qr = pltpu.roll(kvq[:, 256:512], 192, 1)
-        Q[zt] = jnp.where(lane256 < 160, qr, 0.0).astype(BF)
+        qr = jnp.where(lane256 < 160, qr, 0.0)
+        Q[zt] = qr.astype(BF)
+        QT[zt] = jnp.transpose(qr).astype(BF)
         src = KV.at[h, zt, y]
         kv1.append(send(src, src, P1))
         kv2.append(send(src, src, P2))
@@ -260,24 +263,6 @@
         kv1[k].wait_recv()
         got = KV.at[p1h, order[k], p1y]
         kv3.append(send(got, got, P2))
-
-    project(0)
-    token_step(1)
-    f_forward(0)
-    project(1)
-    kv_forward(0)
-    token_step(2)
-    project(2)
-    kv_forward(1)
-    token_step(3)
-    f_line(1)
-    project(3)
-    kv_forward(2)
-    kv_forward(3)
-    f_line(2)
-    f_plane(1)
-    for cp in kv2 + kv3:
-        cp.wait_recv()
 
     scale = HEAD_DIM ** -0.5
     ends = []
@@ -295,52 +280,86 @@
     def rowpos(zt):
         return (h * 8 + zt * 2 + y) * 256
 
-    def fwd_tile(zt, _):
-        qt = h * 8 + zt * 2 + y
-        lo = jnp.maximum(qt - 8, 0)
-        num = qt + 1 - lo
-        qpos = qt * 256 + lax.broadcasted_iota(jnp.int32, (256, 1), 0)
-        seg = seg_of(qpos)
-        q = Q[zt]
-
-        def score(j, ml):
-            m, l = ml
-            kt = lo + j
-            kh, kz, ky = lax.div(kt, 8), lax.rem(lax.div(kt, 2), 4), lax.rem(kt, 2)
-            s = nt(q, KV[kh, kz, ky, :, 0:256]) * scale
-            kpos = kt * 256 + lax.broadcasted_iota(jnp.int32, (256, 256), 1)
-            ok = (kpos >= seg) & (kpos <= qpos)
-            s = jnp.where(ok, s, -1e30)
-            mn = jnp.maximum(m, jnp.max(s, axis=-1, keepdims=True))
+    def pair_range(kt):
+        base = kt - h * 8 - y
+        zlo = jnp.maximum(lax.div(base + 33, 2) - 16, 0)
+        zhi = jnp.minimum(lax.div(base + 40, 2) - 16, 3) + 1
+        return zlo, zhi
+
+    def allowed(kt, zq):
+        kpos = kt * 256 + lax.broadcasted_iota(jnp.int32, (256, 1), 0)
+        qpos = (h * 8 + zq * 2 + y) * 256 + lax.broadcasted_iota(jnp.int32, (1, 256), 1)
+        return (kpos >= seg_of(qpos)) & (kpos <= qpos)
+
+    def absorb(gh, kz, gy):
+        kt = gh * 8 + kz * 2 + gy
+        zlo, zhi = pair_range(kt)
+        TS[...] = jnp.transpose(KV[gh, kz, gy, :, 128:384].astype(F32)).astype(BF)
+        kk = KV.at[gh, kz, gy]
+
+        def one(zq, _):
+            s = jnp.where(allowed(kt, zq), nn(kk[:, 0:256], QT[zq]) * scale, -1e30)
+            m = MS[zq, 0:1, :]
+            mn = jnp.maximum(m, jnp.max(s, axis=0, keepdims=True))
             f = jnp.exp(m - mn)
-            p = jnp.where(ok, jnp.exp(s - mn), 0.0)
-            O[zt] = O[zt] * f + nn(p.astype(BF), KV[kh, kz, ky, :, 128:384])
-            return mn, l * f + jnp.sum(p, axis=-1, keepdims=True)
-
-        O[zt] = jnp.zeros((256, 256), F32)
-        start = (jnp.full((256, 1), -1e30, F32), jnp.zeros((256, 1), F32))
-        m, l = lax.fori_loop(0, num, score, start)
-        o = O[zt] / l
-        O[zt] = o
-        LS[zt] = jnp.broadcast_to(m + jnp.log(l), (256, 128))
-        a = pltpu.roll(o, 224, 1).astype(BF)
-        As[zt] = a.reshape(2, 128, 256)
+            p = jnp.exp(s - mn)
+            MS[zq, 0:1, :] = mn
+            MS[zq, 1:2, :] = MS[zq, 1:2, :] * f + jnp.sum(p, axis=0, keepdims=True)
+            OT[zq] = OT[zq] * f + nn(TS[...], p.astype(BF))
+            return 0
+
+        lax.fori_loop(zlo, zhi, one, 0)
         return 0
 
+    def group(gh, gy):
+        lax.fori_loop(0, 4, lambda kz, _: absorb(gh, kz, gy), 0)
+
+    OT[...] = jnp.zeros((4, 256, 256), F32)
+    MS[:, 0:1, :] = jnp.full((4, 1, 256), -1e30, F32)
+    MS[:, 1:2, :] = jnp.zeros((4, 1, 256), F32)
+
+    def finish(zt):
+        m, l = MS[zt, 0:1, :], MS[zt, 1:2, :]
+        o = OT[zt] / l
+        OT[zt] = o
+        MS[zt, 0:1, :] = m + jnp.log(l)
+        turned = jnp.concatenate([o[32:256, :], o[0:32, :]], axis=0)
+        As[zt] = jnp.transpose(turned).astype(BF).reshape(2, 128, 256)
+
+    project(0)
+    token_step(1)
+    f_forward(0)
+    project(1)
+    token_step(2)
+    f_line(1)
+    project(2)
+    kv_forward(0)
+    token_step(3)
+    f_line(2)
+    project(3)
+    kv_forward(1)
+    kv_forward(2)
+    kv_forward(3)
+    f_plane(1)
+    group(h, y)
+    f_plane(2)
+    group(p1h, p1y)
+    f_forward(1)
+    for cp in kv2:
+        cp.wait_recv()
+    group(p2h, p2y)
+    for cp in kv3:
+        cp.wait_recv()
+    group(hx, yx)
+    f_forward(2)
     asend = []
     for k in (1, 2, 3, 0):
         zt = zs[k]
-        fwd_tile(zt, 0)
+        finish(zt)
         for cc in (c, sib):
             if k == 0 and cc is c:
                 continue
             asend.append(send(As.at[zt, cc], A.at[t], dev(h, zt, y, cc)))
-        if k == 1:
-            f_plane(2)
-        if k == 2:
-            f_forward(1)
-        if k == 3:
-            f_forward(2)
     A[t] = As[z, c]
 
     f_last(0)
@@ -374,9 +393,7 @@
 
     def norm2(i, _):
         rows = pl.ds(pl.multiple_of(i * 32, 32), 32)
-        n2, r2 = stats(MID[rows, :])
-        N2[rows, :] = n2
-        RR[rows, :] = jnp.broadcast_to(r2, (32, 128))
+        n2, _ = stats(MID[rows, :])
         H2[rows, :] = (n2 * vec[5:6, :] + vec[6:7, :]).astype(BF)
         return 0
 
@@ -498,28 +515,27 @@
         VR[103:104, cols] = jnp.sum(de.astype(F32), axis=0, keepdims=True)
 
     halves(act_half)
+    def back_half(i, cols):
+        f0, f1w = F[1, 0, i].reshape(640, 640), F[1, 1, i].reshape(640, 640)
+        EX[:, cols] = nt(DE[:, 0:640], f0) + nt(DE[:, 640:1280], f1w)
+
     left([cp for row in fz + flast for cp in row] + f1 + f2a + f2b + fs)
     outer(H2, DE, F.at[2])
     rs_a(1)
-
-
-    def back_half(i, cols):
-        f0, f1w = F[1, 0, i].reshape(640, 640), F[1, 1, i].reshape(640, 640)
-        EX[:, cols] = nt(DE[:, 0:640], f0) + nt(DE[:, 640:1280], f1w)
-
     rs_b(2)
     halves(back_half)
 
     def norm2_back(i, _):
         rows = pl.ds(pl.multiple_of(i * 32, 32), 32)
-        dh2, n2 = EX[rows, :], N2[rows, :]
+        dh2 = EX[rows, :]
+        n2, r2 = stats(MID[rows, :])
         VR[101:102, :] += jnp.sum(dh2 * n2, axis=0, keepdims=True)
         VR[102:103, :] += jnp.sum(dh2, axis=0, keepdims=True)
         wv = dh2 * vec[5:6, :]
-        dmid = CI[rows, :].astype(F32) + RR[rows, 0:1] * (
+        dmid = CI[rows, :].astype(F32) + r2 * (
             wv - jnp.mean(wv, axis=-1, keepdims=True) - n2 * jnp.mean(wv * n2, axis=-1, keepdims=True)
         )
-        MID[rows, :] = dmid
+        EX[rows, :] = dmid
         gb = dmid.astype(BF)
         GB[rows, :] = gb
         VR[100:101, :] += jnp.sum(gb.astype(F32), axis=0, keepdims=True)
@@ -556,34 +572,20 @@
         lax.fori_loop(0, 2, one, 0)
         return 0
 
-    rs_b(1)
     lax.fori_loop(0, 8, outo, 0)
     rs_a(0)
-
-    rx.wait_recv()
-    pm = perm[pl.ds(h * 16 + b, 1), :]
-    om0 = jnp.where(pm == b * 128 + i_sub, 1.0, 0.0).astype(BF)
-    om1 = jnp.where(pm == (16 + b) * 128 + i_sub, 1.0, 0.0).astype(BF)
-
-    def mix_half(i, cols):
-        mixed_out[:, cols] = (tn(om0, RES[0, :, cols]) + tn(om1, RES[1, :, cols])).astype(BF)
-
-    halves(mix_half)
-    rs_b(0)
-
 
     for cp in dos:
         cp.wait_recv()
     left(kv1 + kv2 + kv3)
 
-    lane128 = lax.broadcasted_iota(jnp.int32, (256, 128), 1)
-
     def prep(zt, _):
-        do = pltpu.roll(DOr[zt].reshape(256, 256).astype(F32), 32, 1)
-        DOs[zt] = do.astype(BF)
-        agree = jnp.sum(do * O[zt], axis=-1, keepdims=True)
-        both = jnp.where(lane128 == 0, LS[zt], jnp.where(lane128 == 1, agree, 0.0))
-        ST[zt] = jnp.transpose(both)[0:8, :]
+        do = DOr[zt].reshape(256, 256).astype(F32)
+        DOs[zt] = pltpu.roll(do, 32, 1).astype(BF)
+        dt = jnp.transpose(do)
+        dt = jnp.concatenate([dt[224:256, :], dt[0:224, :]], axis=0)
+        DOT[zt] = dt.astype(BF)
+        MS[zt, 1:2, :] = jnp.sum(dt * OT[zt], axis=0, keepdims=True)
         DQ[zt] = jnp.zeros((256, 256), F32)
         return 0
 
@@ -591,29 +593,20 @@
 
     def key_tile(kh, kz, ky):
         kt = kh * 8 + kz * 2 + ky
-        base = kt - h * 8 - y
-        zlo = jnp.maximum(lax.div(base + 33, 2) - 16, 0)
-        zhi = jnp.minimum(lax.div(base + 40, 2) - 16, 3) + 1
+        zlo, zhi = pair_range(kt)
         DK[...] = jnp.zeros((256, 256), F32)
         DV[...] = jnp.zeros((256, 256), F32)
-        kk = KV[kh, kz, ky, :, 0:256]
-        vv = KV[kh, kz, ky, :, 128:384]
-        kpos = kt * 256 + lax.broadcasted_iota(jnp.int32, (256, 1), 0)
+        tile = KV.at[kh, kz, ky]
+        TS[...] = jnp.transpose(tile[:, 0:256].astype(F32)).astype(BF)
 
         def one(zq, _):
-            q = Q[zq]
-            do = DOs[zq]
-            qpos = (h * 8 + zq * 2 + y) * 256 + lax.broadcasted_iota(jnp.int32, (1, 256), 1)
-            seg = seg_of(qpos)
-            st = ST[zq]
-            s = nt(kk, q) * scale
-            ok = (kpos >= seg) & (kpos <= qpos)
-            p = jnp.where(ok, jnp.exp(jnp.where(ok, s - st[0:1, :], 0.0)), 0.0)
-            dp = nt(vv, do)
-            ds = (p * (dp - st[1:2, :])).astype(BF)
-            DK[...] += nn(ds, q)
-            DV[...] += nn(p.astype(BF), do)
-            DQ[zq] += tn(ds, kk)
+            s = nn(tile[:, 0:256], QT[zq]) * scale
+            p = jnp.exp(jnp.where(allowed(kt, zq), s - MS[zq, 0:1, :], -1e30))
+            dp = nn(tile[:, 128:384], DOT[zq])
+            ds = (p * (dp - MS[zq, 1:2, :])).astype(BF)
+            DK[...] += nn(ds, Q[zq])
+            DV[...] += nn(p.astype(BF), DOs[zq])
+            DQ[zq] += nn(TS[...], ds)
             return 0
 
         lax.fori_loop(zlo, zhi, one, 0)
@@ -625,34 +618,42 @@
 
     dk0, dk1, dk2 = {}, {}, {}
     turn = (1, 2, 3, 0)
-    for k in turn:
+
+    def far_tiles(k):
         kz = zs[k]
         key_tile(hx, kz, yx)
         dk1[k] = send(KV.at[hx, kz, yx], DKVr.at[1, kz], P2)
         key_tile(p2h, kz, p2y)
         dk0[k] = send(KV.at[p2h, kz, p2y], DKVr.at[0, kz], P2)
-    rs_c(2)
-    for k in turn:
+
+    def near_tile(k):
         kz = zs[k]
         key_tile(p1h, kz, p1y)
         dk1[k].wait_recv()
         KV[p1h, kz, p1y] = (KV[p1h, kz, p1y].astype(F32) + DKVr[1, kz].astype(F32)).astype(BF)
         dk2[k] = send(KV.at[p1h, kz, p1y], DKVr.at[2, kz], P1)
-    rs_d(2)
-    rs_c(1)
 
     def own_tile(kz, _):
         key_tile(h, kz, y)
         return 0
 
+    rs_c(2)
+    far_tiles(1)
+    far_tiles(2)
+    near_tile(1)
+    far_tiles(3)
+    near_tile(2)
+    far_tiles(0)
+    rs_b(1)
+    near_tile(3)
+    near_tile(0)
+    rs_d(2)
     lax.fori_loop(0, 4, own_tile, 0)
-    rs_c(0)
-    rs_e(2)
-    rs_d(1)
+    rs_b(0)
 
     def join(zt, _):
         dkv = KV[h, zt, y].astype(F32) + DKVr[0, zt].astype(F32) + DKVr[2, zt].astype(F32)
-        dq = pltpu.roll(jnp.where(lane256 < 160, DQ[zt] * scale, 0.0), 64, 1)
+        dq = pltpu.roll(jnp.where(lane256 < 160, jnp.transpose(DQ[zt]) * scale, 0.0), 64, 1)
         DKVQ[zt, :, 0:256] = dkv[:, 0:256].astype(BF)
         DKVQ[zt, :, 256:384] = (dkv[:, 256:384] + dq[:, 0:128]).astype(BF)
         DKVQ[zt, :, 384:512] = dq[:, 128:256].astype(BF)
@@ -672,24 +673,39 @@
 
         halves(u_half)
 
-        def gain(i, _):
-            rows = pl.ds(pl.multiple_of(lax.rem(i, 2) * 64, 64), 64)
-            n, _ = stats(T[zt, lax.div(i, 2), rows].astype(F32))
-            VR[96:97, :] += jnp.sum(U[zt, lax.div(i, 2), rows].astype(F32) * n, axis=0, keepdims=True)
-            return 0
-
-        lax.fori_loop(0, 4, gain, 0)
         return 0
 
-    us = []
-    for k in turn:
+    def gain_sum(i, _):
+        zt = lax.div(i, 2)
+        rows = pl.ds(pl.multiple_of(lax.rem(i, 2) * 64, 64), 64)
+        n, _ = stats(T[zt, c, rows].astype(F32))
+        VR[96:97, :] += jnp.sum(U[zt, c, rows].astype(F32) * n, axis=0, keepdims=True)
+        return 0
+
+    us, uz = {}, []
+
+    def block_sum(k):
+        us[k].wait_recv()
+        zt = zs[k]
+        U[zt, c] = (U[zt, c].astype(F32) + UR[zt].astype(F32)).astype(BF)
+        if k:
+            uz.append(send(U.at[zt, c], UZ.at[k - 1], dev(h, zt, y, c)))
+
+    for i, k in enumerate(turn):
         dk0[k].wait_recv()
         dk2[k].wait_recv()
         join(zs[k], 0)
         first_grad(zs[k], 0)
-        us.append(send(U.at[zs[k], sib], UR.at[zs[k]], SIB))
-
-    rs_d(0)
+        us[k] = send(U.at[zs[k], sib], UR.at[zs[k]], SIB)
+        if i:
+            block_sum(turn[i - 1])
+        if i == 3:
+            rs_c(1)
+    block_sum(0)
+    rs_c(0)
+    lax.fori_loop(0, 8, gain_sum, 0)
+    rs_e(2)
+    rs_d(1)
     VS[99:100, :] = VS[98:99, :]
     vst = jnp.transpose(VS[...])
     vlane = lax.broadcasted_iota(jnp.int32, (160, 128), 1)
@@ -698,14 +714,6 @@
     colb[rows, :] += jnp.where(vlane == 98, vst[320:480, :], 0.0) + jnp.where(
         vlane == 99, vst[160:320, :], 0.0
     )
-
-    uz = []
-    for i, k in enumerate((1, 2, 3, 0)):
-        us[i].wait_recv()
-        zt = zs[k]
-        U[zt, c] = (U[zt, c].astype(F32) + UR[zt].astype(F32)).astype(BF)
-        if k:
-            uz.append(send(U.at[zt, c], UZ.at[k - 1], dev(h, zt, y, c)))
 
     def head_grad(hh, _):
         g = tn(
@@ -719,9 +727,8 @@
 
     lax.fori_loop(0, 2, head_grad, 0)
     dw1 = send(DW.at[hx, :, yx], DWr.at[1], P2)
-    rs_e(1)
-    rs_e(0)
     dw0 = send(DW.at[p2h, :, p2y], DWr.at[0], P2)
+    rs_d(0)
     dw1.wait_recv()
     DW[p1h, :, p1y] = (DW[p1h, :, p1y].astype(F32) + DWr[1].astype(F32)).astype(BF)
     dw2 = send(DW.at[p1h, :, p1y], DWr.at[2], P1)
@@ -734,6 +741,19 @@
         ).astype(BF)
     dwz = [send(DWz.at[zs[k]], DWh.at[z], dev(h, zs[k], y, c)) for k in range(1, 4)]
     DWh[z] = DWz[z]
+    rs_e(1)
+    rs_e(0)
+
+    rx.wait_recv()
+    pm = perm[pl.ds(h * 16 + b, 1), :]
+    om0 = jnp.where(pm == b * 128 + i_sub, 1.0, 0.0).astype(BF)
+    om1 = jnp.where(pm == (16 + b) * 128 + i_sub, 1.0, 0.0).astype(BF)
+
+    def mix_half(i, cols):
+        mixed_out[:, cols] = (tn(om0, RES[0, :, cols]) + tn(om1, RES[1, :, cols])).astype(BF)
+
+    halves(mix_half)
+
 
     for cp in uz:
         cp.wait_recv()
@@ -745,7 +765,7 @@
             u += UZ[k, rows].astype(F32)
         n, r = stats(tok[rows, :].astype(F32))
         wv = u * vec[0:1, :]
-        gt = MID[rows, :] + r * (
+        gt = EX[rows, :] + r * (
             wv - jnp.mean(wv, axis=-1, keepdims=True) - n * jnp.mean(wv * n, axis=-1, keepdims=True)
         )
         gtok_out[rows, :] = gt.astype(BF)
@@ -808,19 +828,19 @@
     scratch = dict(
         WP=vm((2, 4, 40, 512), F32), FP=vm((2, 3, 40, 640), F32),
         T=vm((4, 2, 128, 1280), BF), H=vm((4, 256, 1280), BF), W=vm((2, 4, 2, 80, 512), BF),
-        KV=vm((2, 4, 2, 256, 384), BF), Q=vm((4, 256, 256), BF), O=vm((4, 256, 256), F32),
+        KV=vm((2, 4, 2, 256, 384), BF), Q=vm((4, 256, 256), BF), QT=vm((4, 256, 256), BF), OT=vm((4, 256, 256), F32),
         F=vm((3,) + fshape, BF), G=vm(fshape, BF), R0=vm((3, 2, 4, 2, 80, 640), BF),
         R1=vm((3, 2, 4, 80, 640), BF), R2=vm((3, 4, 80, 640), BF), R3=vm((3, 3, 80, 640), BF),
         FA=vm((3, 80, 640), F32), FR=vm((3, 40, 640), F32),
         wr=vm((4, 40, 512), F32), wasm=vm((4, 80, 512), F32),
         fr=vm((3, 40, 640), F32),
         colb=vm((1408, 128), F32), vec=vm((16, 1280), F32), bias=vm((8, 512), F32),
-        LS=vm((4, 256, 128), F32), ST=vm((4, 8, 256), F32),
+        MS=vm((4, 8, 256), F32), TS=vm((256, 256), BF),
         A=vm((8, 128, 256), BF), As=vm((4, 2, 128, 256), BF), C=vm((2, 128, 1280), BF),
-        RES=vm((2, 128, 1280), BF), MID=vm((128, 1280), F32), N2=vm((128, 1280), F32), RR=vm((128, 128), F32),
+        RES=vm((2, 128, 1280), BF), MID=vm((128, 1280), F32),
         EX=vm((128, 1280), F32), H2=vm((128, 1280), BF), ACT=vm((128, 1280), BF),
         CI=vm((128, 1280), BF), DE=vm((128, 1280), BF), GB=vm((128, 1280), BF),
-        DOs=vm((4, 256, 256), BF), DOr=vm((4, 2, 128, 256), BF),
+        DOs=vm((4, 256, 256), BF), DOT=vm((4, 256, 256), BF), DOr=vm((4, 2, 128, 256), BF),
         DK=vm((256, 256), F32), DV=vm((256, 256), F32), DQ=vm((4, 256, 256), F32),
         DKVr=vm((3, 4, 256, 384), BF), DKVQ=vm((4, 256, 512), BF), U=vm((4, 2, 128, 1280), BF),
         UR=vm((4, 128, 1280), BF), UZ=vm((3, 128, 1280), BF), VR=vm((128, 1280), F32),

time: 246 us -> 238 us (0.967)
  Pallas kernels: 243 us -> 234 us
    pallas_call x1, Pallas kernels: 240 us -> 231 us  [fast_local(): pl.pallas_call(block_kernel, out_shape=(tokens_out, tokens_out) + (rows,)...]
where the time goes in v3:
time: 238 us
  Pallas kernels  234 us (98%)
    pallas_call x1, Pallas kernels, fast_local(): pl.pallas_call(block_kernel, out_shape=(tokens_out, tokens_out) + (rows,)...  231 us

profile of v3, /device:TPU:0, one launch (start us, length us, event | category | flops | bytes accessed | tf_op | source)
XLA Modules:
  0.0 237.6 jit_solution(17296509457848389892)
XLA Ops:
  0.7 0.0 copy-start.8
  0.7 0.0 copy-start.9
  0.7 0.0 copy-start.4
  0.7 0.0 copy-start.5
  0.7 0.0 copy-start.6
  0.7 0.0 copy-start.7
  0.7 0.0 copy-start.1
  0.7 0.0 copy-start.2
  0.7 0.6 copy-done.8
  1.3 0.0 copy-done.9
  1.3 0.0 copy-done.4
  1.3 0.0 copy-done.5
  1.4 0.0 copy-done.6
  1.4 0.0 copy-done.7
  1.4 0.0 copy-done.1
  1.4 0.0 copy-done.2
  1.4 0.0 copy-done.3
  1.4 0.1 stack.39
  1.5 0.1 copy.45
  1.6 0.6 pad_convert_fusion.vcol
  2.2 231.4 %block.1 = (bf16[128,1280]{1,0:T(8,128)(2,1)}, bf16[128,1280]{1,0:T(8,128)(2,1)}, f32[40,1280]{1,0:T(8,128)}, f32[40,1280]{1,0:T(8,128)}, f32[40,1280]{1,0:T(8,1...) custom-call(bf16[128,1280]{1,0:T(8,128)(2,1)} %tok.1, ...), custom_call_target="tpu_custom_call" | custom-call | flops 12000000000 | bytes 6000000 | tf_op jit(solution)/shard_map/block/pallas_call | solution.py:856
  233.6 2.8 %hand_over.1 = (bf16[128,1280]{1,0:T(8,128)(2,1)}, bf16[128,1280]{1,0:T(8,128)(2,1)}, f32[40,1280]{1,0:T(8,128)}, f32[40,1280]{1,0:T(8,128)}, f32[40,1280]{1,0:T...) custom-call(bf16[128,1280]{1,0:T(8,128)(2,1)} %get-tuple-element.34.refs_0_, ...), custom_call_target="tpu_custom_call" | custom-call | tf_op jit(solution)/shard_map/hand_over/pallas_call | solution.py:870
  236.4 0.7 copy-done
  237.1 0.5 slice_bitcast_fusion
  (2 shorter events, 0.0 us)
Async XLA Ops:
  0.7 0.7 copy-start.8
  0.7 0.7 copy-start.9
  0.7 0.7 copy-start.4
  0.7 0.7 copy-start.5
  0.7 0.7 copy-start.6
  0.7 0.7 copy-start.7
  0.7 0.7 copy-start.1
  0.7 0.7 copy-start.2
  0.7 0.7 copy-start.3
  236.4 0.7 copy-start

commit v4 on v3

--- a/solution.py
+++ b/solution.py
@@ -152,6 +152,7 @@
 
     wa = send(WP.at[sib], wr, SIB)
     fa = send(FP.at[sib], fr, SIB)
+    cx = send(cot, C.at[h], XP)
     T[z, c] = tok[...]
     C[h] = cot[...]
 
@@ -162,7 +163,6 @@
         DWz[k] = wasm[k].astype(BF)
     W[h, z, y] = DWz[z]
     wz = [send(DWz.at[zs[k]], W.at[h, z, y], dev(h, zs[k], y, c)) for k in range(1, 4)]
-    cx = send(cot, C.at[h], XP)
     fa.wait_recv()
     FA[:, pl.ds(pl.multiple_of(c * 40, 8), 40), :] = FP[c]
     FA[:, pl.ds(pl.multiple_of(sib * 40, 8), 40), :] = fr[...]

time: 238 us -> 238 us (level)
  no operation moved by 1% of the time
where the time goes in v4:
time: 238 us; the launch traced here: 237 us
  Pallas kernels  234 us (98%)
    pallas_call x1, Pallas kernels, fast_local(): pl.pallas_call(block_kernel, out_shape=(tokens_out, tokens_out) + (rows,)...  231 us

profile of v4, /device:TPU:0, one launch (start us, length us, event | category | flops | bytes accessed | tf_op | source)
XLA Modules:
  0.0 237.4 jit_solution(16565034010183301703)
XLA Ops:
  0.7 0.0 copy-start.8
  0.7 0.0 copy-start.9
  0.7 0.0 copy-start.4
  0.7 0.0 copy-start.5
  0.7 0.0 copy-start.6
  0.7 0.0 copy-start.7
  0.7 0.0 copy-start.1
  0.7 0.0 copy-start.2
  0.7 0.6 copy-done.8
  1.3 0.0 copy-done.9
  1.3 0.0 copy-done.4
  1.3 0.0 copy-done.5
  1.4 0.0 copy-done.6
  1.4 0.0 copy-done.7
  1.4 0.0 copy-done.1
  1.4 0.0 copy-done.2
  1.4 0.0 copy-done.3
  1.4 0.1 stack.39
  1.5 0.1 copy.45
  1.6 0.6 pad_convert_fusion.vcol
  2.2 231.2 %block.1 = (bf16[128,1280]{1,0:T(8,128)(2,1)}, bf16[128,1280]{1,0:T(8,128)(2,1)}, f32[40,1280]{1,0:T(8,128)}, f32[40,1280]{1,0:T(8,128)}, f32[40,1280]{1,0:T(8,1...) custom-call(bf16[128,1280]{1,0:T(8,128)(2,1)} %tok.1, ...), custom_call_target="tpu_custom_call" | custom-call | flops 12000000000 | bytes 6000000 | tf_op jit(solution)/shard_map/block/pallas_call | solution.py:856
  233.4 2.8 %hand_over.1 = (bf16[128,1280]{1,0:T(8,128)(2,1)}, bf16[128,1280]{1,0:T(8,128)(2,1)}, f32[40,1280]{1,0:T(8,128)}, f32[40,1280]{1,0:T(8,128)}, f32[40,1280]{1,0:T...) custom-call(bf16[128,1280]{1,0:T(8,128)(2,1)} %get-tuple-element.34.refs_0_, ...), custom_call_target="tpu_custom_call" | custom-call | tf_op jit(solution)/shard_map/hand_over/pallas_call | solution.py:870
  236.2 0.7 copy-done
  236.9 0.5 slice_bitcast_fusion
  (2 shorter events, 0.0 us)
Async XLA Ops:
  0.7 0.7 copy-start.8
  0.7 0.7 copy-start.9
  0.7 0.7 copy-start.4
  0.7 0.7 copy-start.5
  0.7 0.7 copy-start.6
  0.7 0.7 copy-start.7
  0.7 0.7 copy-start.1
  0.7 0.7 copy-start.2
  0.7 0.7 copy-start.3
  236.2 0.7 copy-start
